TPU v7x, 32 devices: a whole 2x2x4 slice. The times are simulated.
32 devices in a mesh: lag: 2 (over y), row: 16 (over z, x, core).
Axes of the slice: x: 2, y: 2, z: 4, core: 2. Of those that a mesh axis runs over, the one named last changes fastest.
Arguments:
- lag_matrices: bfloat16 [8, 8192, 8192], P('lag', 'row'), may hold values from -0.0234375 to 0.0234375
- history: bfloat16 [8, 8192, 256], P('lag', 'row'), may hold values from -6 to 6
- excitation: float32 [4, 8192, 256], P(None, 'row'), may hold values from -6 to 6
- admittance: float32 [8192], P('row'), may hold values from 0.3 to 1.5
- saturation: float32 [8192], P('row'), may hold values from 0.2 to 1
Outputs:
- densities: bfloat16 [4, 8192, 256], P(None, 'row')
All inputs are finite; a program needn't handle non-finite values.
Results may differ from a plain program's by a relative error of at most 0.0023.
Values may be sent and summed in bfloat16 or wider, within the bound.
No kernel may reach another device: no remote copies, remote signals or barrier semaphores. Data moves between devices by JAX's collectives and lax.ppermute only.
A program may use at most 192 MiB of HBM per device.

v0:
```python
import jax
import jax.numpy as jnp
from jax import lax
from jax.sharding import PartitionSpec as P


def load_update(drive, admit_col, satur_col):
    return (admit_col * drive / jnp.sqrt(1.0 + (satur_col * drive) ** 2)).astype(jnp.bfloat16)


def body(lag_matrices, history, excitation, admittance, saturation):
    slot_count = lag_matrices.shape[0]
    step_count = excitation.shape[0]
    lag_index = lax.axis_index("lag")
    admit_col = admittance[:, None]
    satur_col = saturation[:, None]
    archive = lax.all_gather(history, "lag", axis=0, tiled=True)
    archive = lax.all_gather(archive, "row", axis=1, tiled=True)
    results = []
    for step_index in range(step_count):
        own_slots = lax.dynamic_slice_in_dim(archive, lag_index * slot_count, slot_count, 0)
        partial_sum = jnp.einsum(
            "lrm,lmc->rc", lag_matrices, own_slots, preferred_element_type=jnp.float32
        )
        summed = lax.psum(partial_sum, "lag")
        density = load_update(excitation[step_index] - summed, admit_col, satur_col)
        results.append(density)
        if step_index + 1 < step_count:
            full_density = lax.all_gather(density, "row", axis=0, tiled=True)
            archive = jnp.concatenate([full_density[None], archive[:-1]], axis=0)
    return jnp.stack(results)


def solution(mesh):
    placed = (
        P("lag", "row", None),
        P("lag", "row", None),
        P(None, "row", None),
        P("row"),
        P("row"),
    )
    return jax.shard_map(
        body, mesh=mesh, in_specs=placed, out_specs=P(None, "row", None), check_vma=False
    )
```

profile of v0, /device:TPU:0, one launch (start us, length us, event | category | flops | bytes accessed | tf_op | source)
XLA Modules:
  0.0 600.8 jit_solution(13560275325558373227)
XLA Ops:
  7.3 37.5 %all-gather.6.cloned.1.call-done = bf16[8,512,256]{2,1,0:T(8,128)(2,1)} async-done(((bf16[4,512,256]{2,1,0:T(8,128)(2,1)}), bf16[8,512,256]{2,1,0:T(8,128)(2,1)}) %all-gather.6.cloned.1.call-update) | async-done | bytes 2097168 | tf_op jit(solution)/shard_map/all_gather | solution.py:17
  44.8 3.9 copy.13
  48.8 168.1 %all-gather.8.cloned.1.call-done = bf16[8,8192,256]{1,2,0:T(8,128)(2,1)} async-done(((bf16[8,512,256]{1,2,0:T(8,128)(2,1)}), bf16[8,8192,256]{1,2,0:T(8,128)(2,1)}) %all-gather.8.cloned.1.call-update) | async-done | bytes 33554448 | tf_op jit(solution)/shard_map/all_gather | solution.py:18
  216.9 18.9 %fusion.11 = f32[512,256]{0,1:T(8,128)} fusion(bf16[4,512,8192]{2,1,0:T(8,128)(2,1)} %param.5, bf16[8,8192,256]{1,2,0:T(8,128)(2,1)} %all-gather.8.cloned.1.call-done, s32[]{:T(128)S(6)} %select_n.2), kind=kOutput, calls=%fused_computation.14 | convolution fusion | flops 8589934592 | bytes 50855940 | tf_op jit(solution)/shard_map/lrm,lmc->rc/dot_general | solution.py:22
  235.9 1.2 fusion.30
  237.1 1.2 copy.18
  238.3 26.2 %all-reduce.5.cloned.1.call-done = f32[512,256]{0,1:T(8,128)} async-done(((f32[512,256]{0,1:T(8,128)}), f32[512,256]{0,1:T(8,128)}) %all-reduce.5.cloned.1.call-update) | async-done | bytes 524304 | tf_op jit(solution)/shard_map/psum | solution.py:25
  264.6 1.9 multiply_convert_fusion.3
  266.5 20.2 %slice.28 = bf16[7,8192,256]{1,2,0:T(8,128)(2,1)} slice(bf16[8,8192,256]{1,2,0:T(8,128)(2,1)} %all-gather.8.cloned.1.call-done), slice={[0:7], [0:8192], [0:256]} | slice | bytes 58720256 | tf_op jit(solution)/shard_map/slice | solution.py:30
  286.7 33.3 %all-gather.10.cloned.1.call-done = bf16[8192,256]{0,1:T(8,128)(2,1)} async-done(((bf16[512,256]{0,1:T(8,128)(2,1)}), bf16[8192,256]{0,1:T(8,128)(2,1)}) %all-gather.10.cloned.1.call-update) | async-done | bytes 4194320 | tf_op jit(solution)/shard_map/all_gather | solution.py:29
  320.0 18.9 %fusion.17 = f32[512,256]{0,1:T(8,128)} fusion(bf16[4,512,8192]{2,1,0:T(8,128)(2,1)} %param.5, s32[]{:T(128)S(6)} %select_n.2, bf16[1,8192,256]{1,2,0:T(8,128)(2,1)} %bitcast.46, bf16[7,8192,256]{1,2,0:T(8,128)(2,1)} %slice.28), kind=kOutput, calls=%fused_computation.16 | convolution fusion | flops 8598323200 | bytes 67633152 | tf_op jit(solution)/shard_map/lrm,lmc->rc/dot_general | solution.py:22
  339.2 26.7 %all-reduce.7.cloned.1.call-done = f32[512,256]{0,1:T(8,128)} async-done(((f32[512,256]{0,1:T(8,128)}), f32[512,256]{0,1:T(8,128)}) %all-reduce.7.cloned.1.call-update) | async-done | bytes 524304 | tf_op jit(solution)/shard_map/psum | solution.py:25
  365.9 1.9 multiply_convert_fusion.2
  367.8 53.3 %all-gather.12.cloned.1.call-done = bf16[8192,256]{0,1:T(8,128)(2,1)} async-done(((bf16[512,256]{0,1:T(8,128)(2,1)}), bf16[8192,256]{0,1:T(8,128)(2,1)}) %all-gather.12.cloned.1.call-update) | async-done | bytes 4194320 | tf_op jit(solution)/shard_map/all_gather | solution.py:29
  421.1 22.8 %fusion = bf16[8,8192,256]{1,2,0:T(8,128)(2,1)} fusion(bf16[7,8192,256]{1,2,0:T(8,128)(2,1)} %slice.28, bf16[1,8192,256]{1,2,0:T(8,128)(2,1)} %bitcast.47, bf16[1,8192,256]{1,2,0:T(8,128)(2,1)} %bitcast.48), kind=kLoop, calls=%fused_computation.1 | loop fusion | flops 33554432 | bytes 71303168 | tf_op jit(solution)/shard_map/concatenate | solution.py:30
  443.9 18.9 %fusion.14 = f32[512,256]{0,1:T(8,128)} fusion(bf16[4,512,8192]{2,1,0:T(8,128)(2,1)} %param.5, bf16[8,8192,256]{1,2,0:T(8,128)(2,1)} %fusion, s32[]{:T(128)S(6)} %select_n.2), kind=kOutput, calls=%fused_computation.15 | convolution fusion | flops 8589934592 | bytes 50855940 | tf_op jit(solution)/shard_map/lrm,lmc->rc/dot_general | solution.py:22
  463.1 26.7 %all-reduce.9.cloned.1.call-done = f32[512,256]{0,1:T(8,128)} async-done(((f32[512,256]{0,1:T(8,128)}), f32[512,256]{0,1:T(8,128)}) %all-reduce.9.cloned.1.call-update) | async-done | bytes 524304 | tf_op jit(solution)/shard_map/psum | solution.py:25
  489.8 1.9 multiply_convert_fusion.1
  491.9 20.2 %slice.29 = bf16[7,8192,256]{1,2,0:T(8,128)(2,1)} slice(bf16[8,8192,256]{1,2,0:T(8,128)(2,1)} %fusion), slice={[0:7], [0:8192], [0:256]} | slice | bytes 58720256 | tf_op jit(solution)/shard_map/slice | solution.py:30
  512.1 33.3 %all-gather.14.cloned.1.call-done = bf16[8192,256]{0,1:T(8,128)(2,1)} async-done(((bf16[512,256]{0,1:T(8,128)(2,1)}), bf16[8192,256]{0,1:T(8,128)(2,1)}) %all-gather.14.cloned.1.call-update) | async-done | bytes 4194320 | tf_op jit(solution)/shard_map/all_gather | solution.py:29
  545.4 19.3 %fusion.20 = f32[512,256]{0,1:T(8,128)} fusion(bf16[4,512,8192]{2,1,0:T(8,128)(2,1)} %param.5, s32[]{:T(128)S(6)} %select_n.2, bf16[1,8192,256]{1,2,0:T(8,128)(2,1)} %bitcast.52, bf16[7,8192,256]{1,2,0:T(8,128)(2,1)} %slice.29), kind=kOutput, calls=%fused_computation.17 | convolution fusion | flops 8598323200 | bytes 67633152 | tf_op jit(solution)/shard_map/lrm,lmc->rc/dot_general | solution.py:22
  564.9 26.7 %all-reduce.11.cloned.1.call-done = f32[512,256]{0,1:T(8,128)} async-done(((f32[512,256]{0,1:T(8,128)}), f32[512,256]{0,1:T(8,128)}) %all-reduce.11.cloned.1.call-update) | async-done | bytes 524304 | tf_op jit(solution)/shard_map/psum | solution.py:25
  591.6 1.2 fusion.23
  593.0 1.3 copy.17
  (36 shorter events, 2.1 us)
Async XLA Ops:
  6.5 38.2 %all-gather.6.cloned.1.call-start = ((), (), s32[]{:S(2)}) async-start(), calls=%async_computation | async-start | bytes 3145728 | tf_op jit(solution)/shard_map/all_gather | solution.py:17
  7.3 209.7 %all-gather.8.cloned.1.call-start = ((), (), s32[]{:S(2)}) async-start(), calls=%async_computation.1 | async-start | bytes 35651584 | tf_op jit(solution)/shard_map/all_gather | solution.py:18
  48.7 215.9 %all-reduce.5.cloned.1.call-start = ((), (), s32[]{:S(2)}) async-start(), calls=%async_computation.2 | async-start | bytes 1048576 | tf_op jit(solution)/shard_map/psum | solution.py:25
  48.8 187.1 %copy-start.3 = (f32[4,512,256]{2,1,0:T(8,128)S(1)}, f32[4,512,256]{2,1,0:T(8,128)}, u32[]{:S(2)}) copy-start(f32[4,512,256]{2,1,0:T(8,128)} %param.7) | copy-start | bytes 6291460
  48.8 215.8 %copy-start.5 = (f32[512]{0:T(512)S(1)}, f32[512]{0:T(512)}, u32[]{:S(2)}) copy-start(f32[512]{0:T(512)} %param.9) | copy-start | bytes 6148
  48.8 215.8 %copy-start.6 = (f32[512]{0:T(512)S(1)}, f32[512]{0:T(512)}, u32[]{:S(2)}) copy-start(f32[512]{0:T(512)} %param.8) | copy-start | bytes 6148
  235.8 84.2 %all-gather.10.cloned.1.call-start = ((), (), s32[]{:S(2)}) async-start(), calls=%async_computation.3 | async-start | bytes 4456448 | tf_op jit(solution)/shard_map/all_gather | solution.py:29
  266.5 99.4 %all-reduce.7.cloned.1.call-start = ((), (), s32[]{:S(2)}) async-start(), calls=%async_computation.4 | async-start | bytes 1048576 | tf_op jit(solution)/shard_map/psum | solution.py:25
  338.9 82.2 %all-gather.12.cloned.1.call-start = ((), (), s32[]{:S(2)}) async-start(), calls=%async_computation.5 | async-start | bytes 4456448 | tf_op jit(solution)/shard_map/all_gather | solution.py:29
  367.8 122.0 %all-reduce.9.cloned.1.call-start = ((), (), s32[]{:S(2)}) async-start(), calls=%async_computation.6 | async-start | bytes 1048576 | tf_op jit(solution)/shard_map/psum | solution.py:25
  462.9 82.6 %all-gather.14.cloned.1.call-start = ((), (), s32[]{:S(2)}) async-start(), calls=%async_computation.7 | async-start | bytes 4456448 | tf_op jit(solution)/shard_map/all_gather | solution.py:29
  491.7 99.9 %all-reduce.11.cloned.1.call-start = ((), (), s32[]{:S(2)}) async-start(), calls=%async_computation.8 | async-start | bytes 1048576 | tf_op jit(solution)/shard_map/psum | solution.py:25
  545.4 19.3 %copy-start.4 = (f32[1,512,256]{2,1,0:T(8,128)S(1)}, f32[1,512,256]{2,1,0:T(8,128)}, u32[]{:S(2)}) copy-start(f32[1,512,256]{2,1,0:T(8,128)} %get-tuple-element.5) | copy-start | bytes 1572868
  545.4 47.4 %copy-start = (bf16[512,256]{0,1:T(8,128)(2,1)S(1)}, bf16[512,256]{0,1:T(8,128)(2,1)}, u32[]{:S(2)}) copy-start(bf16[512,256]{0,1:T(8,128)(2,1)} %multiply_convert_fusion.3) | copy-start | bytes 786436
  545.4 47.4 %copy-start.1 = (bf16[512,256]{0,1:T(8,128)(2,1)S(1)}, bf16[512,256]{0,1:T(8,128)(2,1)}, u32[]{:S(2)}) copy-start(bf16[512,256]{0,1:T(8,128)(2,1)} %multiply_convert_fusion.2) | copy-start | bytes 786436
  545.4 47.4 %copy-start.2 = (bf16[512,256]{0,1:T(8,128)(2,1)S(1)}, bf16[512,256]{0,1:T(8,128)(2,1)}, u32[]{:S(2)}) copy-start(bf16[512,256]{0,1:T(8,128)(2,1)} %multiply_convert_fusion.1) | copy-start | bytes 786436
Sparse Core Ops, SparseCore 0:
  8.9 35.8 all-gather.5
  48.8 168.0 all-gather.7
  235.9 28.5 all-reduce.4
  266.8 53.2 all-gather.9
  339.1 26.7 all-reduce.6
  367.9 53.2 all-gather.11
  463.0 26.7 all-reduce.8
  492.2 53.2 all-gather.13
  564.8 26.7 all-reduce.10
where the time goes:
time: 601 us
  waiting for transfers between devices  433 us (72%)
  matrix products  75.9 us (13%)
  local copies, waits for them, and re-layouts  48.7 us (8%)
  other arithmetic  29.8 us (5%)
  between operations  13.3 us (2%)
    all_gather x1, waiting for transfers between devices, body(): archive = lax.all_gather(archive, 'row', axis=1, tiled=True)  168 us
    all_gather x3, waiting for transfers between devices, body(): full_density = lax.all_gather(density, 'row', axis=0, tiled=True)  120 us
    psum x4, waiting for transfers between devices, body(): summed = lax.psum(partial_sum, 'lag')  106 us
    dot_general x4, matrix products, body(): jnp.einsum('lrm,lmc->rc', lag_matrices, own_slots, preferred_element_type...  75.9 us
    slice x2, local copies, waits for them, and re-layouts, body(): archive = jnp.concatenate([full_density[None], archive[:-1]], axis=0)  40.4 us
    all_gather x1, waiting for transfers between devices, body(): archive = lax.all_gather(history, 'lag', axis=0, tiled=True)  37.5 us
    concatenate x1, other arithmetic, body(): archive = jnp.concatenate([full_density[None], archive[:-1]], axis=0)  22.8 us
  transfers between devices with their start and end apart: 9, of which 9 were waited for; matrix products, arithmetic and copies ran while one was open for 7% of the time, Pallas kernels for 0%

commit v1 on v0

--- a/solution.py
+++ b/solution.py
@@ -1,14 +1,250 @@
+import functools
+
 import jax
 import jax.numpy as jnp
 from jax import lax
+from jax.experimental import pallas as pl
+from jax.experimental.pallas import tpu as pltpu
 from jax.sharding import PartitionSpec as P
+
+VMEM_LIMIT = 40 * 1024 * 1024
 
 
 def load_update(drive, admit_col, satur_col):
     return (admit_col * drive / jnp.sqrt(1.0 + (satur_col * drive) ** 2)).astype(jnp.bfloat16)
 
 
-def body(lag_matrices, history, excitation, admittance, saturation):
+def ring_of(members):
+    pairs = [(m, m + 1) for m in range(0, members, 2)]
+    cycle = pairs[0::2] + pairs[1::2][::-1]
+    return [m for pair in cycle for m in pair]
+
+
+def place_in_ring(member, members):
+    pair, core = member // 2, member % 2
+    up, across = pair // 2, pair % 2
+    return 2 * (up + across * (members // 2 - 1 - 2 * up)) + core
+
+
+def dot(a, b):
+    return jnp.dot(a, b, preferred_element_type=jnp.float32)
+
+
+def params():
+    return pltpu.CompilerParams(vmem_limit_bytes=VMEM_LIMIT)
+
+
+def cost(z_blocks, rows, unknowns, columns, products, h_blocks):
+    return pl.CostEstimate(
+        flops=2 * products * rows * unknowns * columns,
+        bytes_accessed=2 * z_blocks * rows * unknowns + 2 * h_blocks * unknowns * columns,
+        transcendentals=0,
+    )
+
+
+def first_kernel(slots, z_ref, h_ref, out_ref):
+    total = dot(z_ref[0], h_ref[0])
+    for slot in range(1, slots):
+        total += dot(z_ref[slot], h_ref[slot])
+
+    @pl.when(pl.program_id(0) == 0)
+    def _():
+        out_ref[...] = total
+
+    @pl.when(pl.program_id(0) > 0)
+    def _():
+        out_ref[...] += total
+
+
+def first_products(members, z, h):
+    slots, rows, unknowns = z.shape
+    columns = h.shape[-1]
+    depth, place = unknowns // members, functools.partial(place_in_ring, members=members)
+    return pl.pallas_call(
+        functools.partial(first_kernel, slots),
+        grid=(members,),
+        in_specs=[
+            pl.BlockSpec((slots, rows, depth), lambda k: (0, 0, k)),
+            pl.BlockSpec((slots, depth, columns), lambda k: (0, place(k), 0)),
+        ],
+        out_specs=pl.BlockSpec((rows, columns), lambda k: (0, 0)),
+        out_shape=jax.ShapeDtypeStruct((rows, columns), jnp.float32),
+        compiler_params=params(),
+        cost_estimate=cost(slots, rows, unknowns, columns, slots, slots),
+    )(z, h)
+
+
+def later_kernel(slots, steps, *refs):
+    z_refs, h_ref, outs = refs[: slots - 1], refs[slots - 1], refs[slots:]
+    for shift in range(1, steps):
+        total = None
+        for slot in range(slots - shift):
+            term = dot(z_refs[slot + shift - 1][0], h_ref[slot])
+            total = term if total is None else total + term
+        out_ref = outs[shift - 1]
+
+        @pl.when(pl.program_id(0) == 0)
+        def _():
+            out_ref[...] = total
+
+        @pl.when(pl.program_id(0) > 0)
+        def _():
+            out_ref[...] += total
+
+
+def later_products(members, z, h, steps):
+    slots, rows, unknowns = z.shape
+    columns = h.shape[-1]
+    depth, place = unknowns // members, functools.partial(place_in_ring, members=members)
+    whole = pl.BlockSpec((rows, columns), lambda k: (0, 0))
+    products = sum(slots - shift for shift in range(1, steps))
+    return pl.pallas_call(
+        functools.partial(later_kernel, slots, steps),
+        grid=(members,),
+        in_specs=[
+            pl.BlockSpec((1, rows, depth), lambda k, slot=slot: (slot, 0, k))
+            for slot in range(1, slots)
+        ]
+        + [pl.BlockSpec((slots - 1, depth, columns), lambda k: (0, place(k), 0))],
+        out_specs=[whole] * (steps - 1),
+        out_shape=[jax.ShapeDtypeStruct((rows, columns), jnp.float32)] * (steps - 1),
+        compiler_params=params(),
+        cost_estimate=cost(slots - 1, rows, unknowns, columns, products, slots - 1),
+    )(*([z] * (slots - 1)), h)
+
+
+def spread_kernel(count, *refs):
+    z_refs, y_ref, accs, outs = (
+        refs[:count], refs[count], refs[count + 1 : 2 * count + 1], refs[2 * count + 1 :]
+    )
+    for z_ref, acc_ref, out_ref in zip(z_refs, accs, outs):
+        term = dot(z_ref[0], y_ref[...])
+
+        @pl.when(pl.program_id(0) == 0)
+        def _():
+            out_ref[...] = acc_ref[...] + term
+
+        @pl.when(pl.program_id(0) > 0)
+        def _():
+            out_ref[...] += term
+
+
+def spread(members, z, y, accs, first_slot):
+    _, rows, unknowns = z.shape
+    columns = y.shape[-1]
+    depth, place = unknowns // members, functools.partial(place_in_ring, members=members)
+    count = len(accs)
+    whole = pl.BlockSpec((rows, columns), lambda k: (0, 0))
+    return pl.pallas_call(
+        functools.partial(spread_kernel, count),
+        grid=(members,),
+        in_specs=[
+            pl.BlockSpec((1, rows, depth), lambda k, slot=first_slot + i: (slot, 0, k))
+            for i in range(count)
+        ]
+        + [pl.BlockSpec((depth, columns), lambda k: (place(k), 0))]
+        + [whole] * count,
+        out_specs=[whole] * count,
+        out_shape=[jax.ShapeDtypeStruct((rows, columns), jnp.float32)] * count,
+        compiler_params=params(),
+        cost_estimate=cost(count, rows, unknowns, columns, count, 1),
+    )(*([z] * count), y, *accs)
+
+
+def step_kernel(z_ref, y_ref, acc_ref, other_ref, exc_ref, admit_ref, satur_ref, part_ref, dens_ref):
+    k = pl.program_id(0)
+    term = dot(z_ref[0], y_ref[...])
+
+    @pl.when(k == 0)
+    def _():
+        part_ref[...] = acc_ref[...] + term
+
+    @pl.when(k > 0)
+    def _():
+        part_ref[...] += term
+
+    @pl.when(k == pl.num_programs(0) - 1)
+    def _():
+        drive = exc_ref[0] - (part_ref[...] + other_ref[...])
+        dens_ref[...] = load_update(drive, admit_ref[...], satur_ref[...])
+
+
+def step(members, z, y, acc, other, excitation, index, admit_col, satur_col):
+    _, rows, unknowns = z.shape
+    columns = y.shape[-1]
+    depth, place = unknowns // members, functools.partial(place_in_ring, members=members)
+    whole = pl.BlockSpec((rows, columns), lambda k: (0, 0))
+    column = pl.BlockSpec((rows, 1), lambda k: (0, 0))
+    return pl.pallas_call(
+        step_kernel,
+        grid=(members,),
+        in_specs=[
+            pl.BlockSpec((1, rows, depth), lambda k: (0, 0, k)),
+            pl.BlockSpec((depth, columns), lambda k: (place(k), 0)),
+            whole,
+            whole,
+            pl.BlockSpec((1, rows, columns), lambda k: (index, 0, 0)),
+            column,
+            column,
+        ],
+        out_specs=[whole, whole],
+        out_shape=[
+            jax.ShapeDtypeStruct((rows, columns), jnp.float32),
+            jax.ShapeDtypeStruct((rows, columns), jnp.bfloat16),
+        ],
+        compiler_params=params(),
+        cost_estimate=cost(1, rows, unknowns, columns, 1, 1),
+    )(z, y, acc, other, excitation, admit_col, satur_col)
+
+
+def gather_rows(block, axis, members):
+    return lax.all_gather(block, "row", axis=axis, tiled=True, axis_index_groups=[ring_of(members)])
+
+
+def two_group_body(members, lag_matrices, history, excitation, admittance, saturation):
+    slots = lag_matrices.shape[0]
+    steps = excitation.shape[0]
+    is_first = lax.axis_index("lag") == 0
+    admit_col, satur_col = admittance[:, None], saturation[:, None]
+    down, up = [(1, 0)], [(0, 1)]
+
+    incoming = lax.ppermute(history[slots - (steps - 1) :], "lag", up)
+    archive = gather_rows(history, 1, members)
+    first_part = first_products(members, lag_matrices, archive)
+    first_other = lax.ppermute(first_part, "lag", down)
+
+    archive, first_part, incoming = lax.optimization_barrier((archive, first_part, incoming))
+    ahead = gather_rows(incoming[steps - 2], 0, members)
+    parts = later_products(members, lag_matrices, archive, steps)
+
+    density = load_update(excitation[0] - (first_part + first_other), admit_col, satur_col)
+    results = [density]
+
+    fresh = spread(members, lag_matrices, ahead, parts, 0)
+    other = lax.ppermute(fresh[0], "lag", down)
+    accs = [jnp.where(is_first, parts[i], fresh[min(i + 1, steps - 2)]) for i in range(steps - 1)]
+
+    for index in range(1, steps):
+        send = density
+        if steps - 2 - index >= 0:
+            send = jnp.where(is_first, density, incoming[steps - 2 - index])
+        fresh_rows = gather_rows(send, 0, members)
+        part, density = step(
+            members, lag_matrices, fresh_rows, accs[0], other, excitation, index, admit_col, satur_col
+        )
+        results.append(density)
+        if index + 1 < steps:
+            other = lax.ppermute(part, "lag", down)
+            fresh_rows, density = lax.optimization_barrier((fresh_rows, density))
+            accs = spread(members, lag_matrices, fresh_rows, accs[1:], 1)
+
+    early = jnp.stack(results[:-1])
+    early = jnp.where(is_first, early, lax.ppermute(early, "lag", up))
+    last = jnp.where(is_first, results[-1], lax.ppermute(results[-1], "lag", up))
+    return jnp.concatenate([early, last[None]], axis=0)
+
+
+def general_body(lag_matrices, history, excitation, admittance, saturation):
     slot_count = lag_matrices.shape[0]
     step_count = excitation.shape[0]
     lag_index = lax.axis_index("lag")
@@ -32,6 +268,7 @@
 
 
 def solution(mesh):
+    groups, members = mesh.shape["lag"], mesh.shape["row"]
     placed = (
         P("lag", "row", None),
         P("lag", "row", None),
@@ -39,6 +276,15 @@
         P("row"),
         P("row"),
     )
+
+    def body(lag_matrices, history, excitation, admittance, saturation):
+        slots, steps = lag_matrices.shape[0], excitation.shape[0]
+        chosen = general_body
+        depth = lag_matrices.shape[2] // members
+        if groups == 2 and members % 4 == 0 and depth % 128 == 0 and 2 < steps <= slots:
+            chosen = functools.partial(two_group_body, members)
+        return chosen(lag_matrices, history, excitation, admittance, saturation)
+
     return jax.shard_map(
         body, mesh=mesh, in_specs=placed, out_specs=P(None, "row", None), check_vma=False
     )

time: 601 us -> 367 us (0.61)
  waiting for transfers between devices: 433 us -> 140 us
  Pallas kernels: 0 us -> 154 us
  matrix products: 75.9 us -> 0 us
  local copies, waits for them, and re-layouts: 48.7 us -> 28.1 us
  other arithmetic: 29.8 us -> 10 us
  starting transfers between devices: 0.51 us -> 18.8 us
    all_gather x5, waiting for transfers between devices: 325 us -> 106 us  [gather_rows(): lax.all_gather(block, 'row', axis=axis, tiled=True, axis_index_groups=[ri...]
    pallas_call x0 -> x8, Pallas kernels: none -> 154 us  [the longest x3 54 us: spread(): pl.pallas_call(functools.partial(spread_kernel, count), grid=(members,),...]
    psum x4 -> x0, waiting for transfers between devices: 106 us -> none  [body(): summed = lax.psum(partial_sum, 'lag')]
    dot_general x4 -> x0, matrix products: 75.9 us -> none  [body(): jnp.einsum('lrm,lmc->rc', lag_matrices, own_slots, preferred_element_type...]
    slice x3 -> x2, local copies, waits for them, and re-layouts: 41.6 us -> 2.86 us  [the longest x1 1.68 us: two_group_body(): ahead = gather_rows(incoming[steps - 2], 0, members)]
    ppermute x0 -> x7, waiting for transfers between devices: none -> 32.6 us  [the longest x1 14.7 us: two_group_body(): first_other = lax.ppermute(first_part, 'lag', down)]
    unnamed x18 -> x50, local copies, waits for them, and re-layouts: 1.86 us -> 25 us
    concatenate x1, other arithmetic: 22.8 us -> 1.06 us  [two_group_body(): return jnp.concatenate([early, last[None]], axis=0)]
  transfers between devices with their start and end apart: 9 -> 12, of which waited for: 9 -> 6; matrix products, arithmetic and copies ran while one was open for 7% -> 2% of each run, Pallas kernels for 0% -> 35%
where the time goes in v1:
time: 367 us; the launch traced here: 364 us
  Pallas kernels  154 us (42%)
  waiting for transfers between devices  140 us (38%)
  local copies, waits for them, and re-layouts  28.1 us (8%)
  starting transfers between devices  18.8 us (5%)
  between operations  13.4 us (4%)
  other arithmetic  10 us (3%)
    all_gather x5, waiting for transfers between devices, gather_rows(): lax.all_gather(block, 'row', axis=axis, tiled=True, axis_index_groups=[ri...  106 us
    pallas_call x3, Pallas kernels, spread(): pl.pallas_call(functools.partial(spread_kernel, count), grid=(members,),...  54 us
    pallas_call x3, Pallas kernels, step(): pl.pallas_call(step_kernel, grid=(members,), in_specs=[pl.BlockSpec((1, r...  38.6 us
    pallas_call x1, Pallas kernels, later_products(): pl.pallas_call(functools.partial(later_kernel, slots, steps), grid=(membe...  37.9 us
    unnamed x50, local copies, waits for them, and re-layouts  25 us
    pallas_call x1, Pallas kernels, first_products(): pl.pallas_call(functools.partial(first_kernel, slots), grid=(members,), i...  23.5 us
    ppermute x1, waiting for transfers between devices, two_group_body(): first_other = lax.ppermute(first_part, 'lag', down)  14.7 us
    ppermute x1, waiting for transfers between devices, two_group_body(): other = lax.ppermute(fresh[0], 'lag', down)  13.1 us
  transfers between devices with their start and end apart: 12, of which 6 were waited for; matrix products, arithmetic and copies ran while one was open for 2% of the time, Pallas kernels for 35%

profile of v1, /device:TPU:0, one launch (start us, length us, event | category | flops | bytes accessed | tf_op | source)
XLA Modules:
  0.0 364.0 jit_solution(18321088083948498802)
XLA Ops:
  8.5 5.9 %collective-permute-start = (bf16[3,512,256]{2,1,0:T(8,128)(2,1)S(1)}, bf16[3,512,256]{2,1,0:T(8,128)(2,1)}, u32[]{:S(2)}, u32[]{:S(2)}) collective-permute-start(bf16[3,512,256]{2,1,0:T(8,128)(2,1)S(1)} %slice.16), channel_id=1, source_target_pairs={{0,16},{1,17},{2,18},{3,19},{4,20},{5,21},{6,22},{7,23},{8,24},{9,... | collective-permute-start | bytes 2359304 | tf_op jit(solution)/shard_map/ppermute | solution.py:211
  14.4 86.3 %all-gather.7.cloned.1.call-done.h_ref.refs_3_ = bf16[4,8192,256]{2,1,0:T(8,128)(2,1)} async-done(((bf16[4,512,256]{2,1,0:T(8,128)(2,1)}), bf16[4,8192,256]{2,1,0:T(8,128)(2,1)}) %all-gather.7.cloned.1.call-update) | async-done | bytes 16777232 | tf_op jit(solution)/shard_map/all_gather | solution.py:201
  100.7 23.5 %shard_map.55 = f32[512,256]{1,0:T(8,128)S(1)} custom-call(bf16[4,512,8192]{2,1,0:T(8,128)(2,1)} %z_ref.7, bf16[4,8192,256]{2,1,0:T(8,128)(2,1)} %all-gather.7.cloned.1.call-done.h_ref.refs_3_), custom_call_target="tpu_custom_call" | custom-call | flops 8589934592 | bytes 50331648 | tf_op jit(solution)/shard_map/pallas_call | solution.py:63
  127.3 14.7 %collective-permute-done.1 = f32[512,256]{1,0:T(8,128)S(1)} collective-permute-done((f32[512,256]{1,0:T(8,128)S(1)}, f32[512,256]{1,0:T(8,128)S(1)}, u32[]{:S(2)}, u32[]{:S(2)}) %collective-permute-start.1) | collective-permute-done | bytes 524320 | tf_op jit(solution)/shard_map/ppermute | solution.py:214
  142.0 2.0 bitcast_select_fusion.1
  144.1 37.9 %shard_map.56 = (f32[512,256]{1,0:T(8,128)S(1)}, f32[512,256]{1,0:T(8,128)S(1)}, f32[512,256]{1,0:T(8,128)S(1)}) custom-call(bf16[4,512,8192]{2,1,0:T(8,128)(2,1)} %z_ref.7, bf16[4,512,8192]{2,1,0:T(8,128)(2,1)} %z_ref.7, bf16[4,512,8192]{2,1,0:T(8,128)(2,1)} %z_ref.7, bf16[4,8192,256]{2,1,0:T(8,128)(2,1)} %all-gather.7.cloned.1.call-done.h_ref.refs_3_), custom_call_target="tpu_custom_call" | custom-call | flops 12884901888 | bytes 37748736 | tf_op jit(solution)/shard_map/pallas_call | solution.py:101
  182.8 2.4 copy-done.5
  186.2 23.5 %shard_map.57 = (f32[512,256]{1,0:T(8,128)}, f32[512,256]{1,0:T(8,128)S(1)}, f32[512,256]{1,0:T(8,128)S(1)}) custom-call(bf16[4,512,8192]{2,1,0:T(8,128)(2,1)} %z_ref.7, bf16[4,512,8192]{2,1,0:T(8,128)(2,1)} %z_ref.7, bf16[4,512,8192]{2,1,0:T(8,128)(2,1)} %z_ref.7, bf16[8192,256]{1,0:T(8,128)(2,1)S(1)} %bitcast.17, ...), custom_call_target="tpu_custom_call" | custom-call | flops 6442450944 | bytes 29360128 | tf_op jit(solution)/shard_map/pallas_call | solution.py:138
  213.8 13.1 %collective-permute-done.2.other_ref = f32[512,256]{1,0:T(8,128)} collective-permute-done((f32[512,256]{1,0:T(8,128)}, f32[512,256]{1,0:T(8,128)}, u32[]{:S(2)}, u32[]{:S(2)}) %collective-permute-start.2) | collective-permute-done | bytes 524320 | tf_op jit(solution)/shard_map/ppermute | solution.py:224
  226.9 2.2 copy-done.1
  230.1 12.5 %shard_map.58 = (f32[512,256]{1,0:T(8,128)S(1)}, bf16[512,256]{1,0:T(8,128)(2,1)S(1)}) custom-call(bf16[4,512,8192]{2,1,0:T(8,128)(2,1)} %z_ref.7, bf16[8192,256]{1,0:T(8,128)(2,1)S(1)} %copy-done.1, f32[512,256]{1,0:T(8,128)S(1)} %copy-done.7, f32[512,256]{1,0:T(8,128)} %collective-permute-done.2.other_ref, f32[4,512,256]{2,1,0:T(8,128)S(1)} %copy-done, ...), custom_call_target="tpu_custom_call" | custom-call | flops 2147483648 | bytes 12582912 | tf_op jit(solution)/shard_map/pallas_call | solution.py:178
  247.8 2.2 copy-done.2
  250.0 18.7 %shard_map.59 = (f32[512,256]{1,0:T(8,128)S(1)}, f32[512,256]{1,0:T(8,128)S(1)}) custom-call(bf16[4,512,8192]{2,1,0:T(8,128)(2,1)} %z_ref.7, bf16[4,512,8192]{2,1,0:T(8,128)(2,1)} %z_ref.7, bf16[8192,256]{1,0:T(8,128)(2,1)S(1)} %copy-done.2, f32[512,256]{1,0:T(8,128)S(1)} %get-tuple-element.48.refs_3_, f32[512,256]{1,0:T(8,128)S(1)} %get-tuple-element.47.refs_4_), custom_call_target="tpu_custom_call" | custom-call | flops 4294967296 | bytes 20971520 | tf_op jit(solution)/shard_map/pallas_call | solution.py:138
  270.3 9.1 %all-gather.11.cloned.1.call-done.y_ref.refs_1_ = bf16[8192,256]{1,0:T(8,128)(2,1)} async-done(((bf16[512,256]{1,0:T(8,128)(2,1)}), bf16[8192,256]{1,0:T(8,128)(2,1)}) %all-gather.11.cloned.1.call-update) | async-done | bytes 4194320 | tf_op jit(solution)/shard_map/all_gather | solution.py:201
  279.4 2.2 copy-done.3
  282.6 13.0 %shard_map.60 = (f32[512,256]{1,0:T(8,128)S(1)}, bf16[512,256]{1,0:T(8,128)(2,1)}) custom-call(bf16[4,512,8192]{2,1,0:T(8,128)(2,1)} %z_ref.7, bf16[8192,256]{1,0:T(8,128)(2,1)S(1)} %copy-done.3, f32[512,256]{1,0:T(8,128)S(1)} %get-tuple-element.37.acc_ref, f32[512,256]{1,0:T(8,128)S(1)} %copy-done.15, f32[4,512,256]{2,1,0:T(8,128)S(1)} %copy-done, ...), custom_call_target="tpu_custom_call" | custom-call | flops 2147483648 | bytes 12582912 | tf_op jit(solution)/shard_map/pallas_call | solution.py:178
  298.5 4.2 %collective-permute-start.4 = (bf16[3,512,256]{2,1,0:T(8,128)(2,1)}, bf16[3,512,256]{2,1,0:T(8,128)(2,1)}, u32[]{:S(2)}, u32[]{:S(2)}) collective-permute-start(bf16[3,512,256]{2,1,0:T(8,128)(2,1)} %pad_maximum_fusion.1), channel_id=1, source_target_pairs={{0,16},{1,17},{2,18},{3,19},{4,20},{5,21},{6,22},{7,23},{8,24},{9,... | collective-permute-start | bytes 2359304 | tf_op jit(solution)/shard_map/ppermute | solution.py:242
  304.0 2.2 copy-done.4
  307.3 11.9 %shard_map.61.acc_ref = f32[512,256]{1,0:T(8,128)S(1)} custom-call(bf16[4,512,8192]{2,1,0:T(8,128)(2,1)} %z_ref.7, bf16[8192,256]{1,0:T(8,128)(2,1)S(1)} %copy-done.4, f32[512,256]{1,0:T(8,128)S(1)} %copy-done.13), custom_call_target="tpu_custom_call" | custom-call | flops 2147483648 | bytes 12582912 | tf_op jit(solution)/shard_map/pallas_call | solution.py:138
  319.9 10.7 %all-gather.13.cloned.1.call-done.y_ref = bf16[8192,256]{1,0:T(8,128)(2,1)} async-done(((bf16[512,256]{1,0:T(8,128)(2,1)}), bf16[8192,256]{1,0:T(8,128)(2,1)}) %all-gather.13.cloned.1.call-update) | async-done | bytes 4194320 | tf_op jit(solution)/shard_map/all_gather | solution.py:201
  330.7 2.2 copy-done.6
  333.9 13.1 %shard_map.62 = (f32[512,256]{1,0:T(8,128)}, bf16[512,256]{1,0:T(8,128)(2,1)S(1)}) custom-call(bf16[4,512,8192]{2,1,0:T(8,128)(2,1)} %z_ref.7, bf16[8192,256]{1,0:T(8,128)(2,1)S(1)} %copy-done.6, f32[512,256]{1,0:T(8,128)S(1)} %shard_map.61.acc_ref, f32[512,256]{1,0:T(8,128)S(1)} %copy-done.17, f32[4,512,256]{2,1,0:T(8,128)S(1)} %copy-done, ...), custom_call_target="tpu_custom_call" | custom-call | flops 2147483648 | bytes 12582912 | tf_op jit(solution)/shard_map/pallas_call | solution.py:178
  347.0 3.4 collective-permute-start.6
  351.5 4.8 %collective-permute-done.6 = bf16[512,256]{1,0:T(8,128)(2,1)S(1)} collective-permute-done((bf16[512,256]{1,0:T(8,128)(2,1)S(1)}, bf16[512,256]{1,0:T(8,128)(2,1)S(1)}, u32[]{:S(2)}, u32[]{:S(2)}) %collective-permute-start.6) | collective-permute-done | bytes 262176 | tf_op jit(solution)/shard_map/ppermute | solution.py:243
  (75 shorter events, 28.9 us)
Async XLA Ops:
  6.5 94.2 %all-gather.7.cloned.1.call-start = ((), (), s32[]{:S(2)}) async-start(), calls=%async_computation | async-start | bytes 17825792 | tf_op jit(solution)/shard_map/all_gather | solution.py:201
  7.3 175.5 %all-gather.15.cloned.1.call-start = ((), (), s32[]{:S(2)}) async-start(), calls=%async_computation.4 | async-start | bytes 4456448 | tf_op jit(solution)/shard_map/all_gather | solution.py:201
  8.5 133.5 %copy-start = (f32[4,512,256]{2,1,0:T(8,128)S(1)}, f32[4,512,256]{2,1,0:T(8,128)}, u32[]{:S(2)}) copy-start(f32[4,512,256]{2,1,0:T(8,128)} %exc_ref.5) | copy-start | bytes 6291460
  8.5 133.5 %copy-start.23 = (f32[512]{0:T(512)S(1)}, f32[512]{0:T(512)}, u32[]{:S(2)}) copy-start(f32[512]{0:T(512)} %param.8) | copy-start | bytes 6148
  8.5 133.5 %copy-start.24 = (f32[512]{0:T(512)S(1)}, f32[512]{0:T(512)}, u32[]{:S(2)}) copy-start(f32[512]{0:T(512)} %param.9) | copy-start | bytes 6148
  8.5 115.7 %collective-permute-start = (bf16[3,512,256]{2,1,0:T(8,128)(2,1)S(1)}, bf16[3,512,256]{2,1,0:T(8,128)(2,1)}, u32[]{:S(2)}, u32[]{:S(2)}) collective-permute-start(bf16[3,512,256]{2,1,0:T(8,128)(2,1)S(1)} %slice.16), channel_id=1, source_target_pairs={{0,16},{1,17},{2,18},{3,19},{4,20},{5,21},{6,22},{7,23},{8,24},{9,... | collective-permute-start | bytes 2359304 | tf_op jit(solution)/shard_map/ppermute | solution.py:211
  126.0 100.9 %all-gather.9.cloned.1.call-start = ((), (), s32[]{:S(2)}) async-start(), calls=%async_computation.1 | async-start | bytes 4456448 | tf_op jit(solution)/shard_map/all_gather | solution.py:201
  126.0 16.0 %collective-permute-start.1 = (f32[512,256]{1,0:T(8,128)S(1)}, f32[512,256]{1,0:T(8,128)S(1)}, u32[]{:S(2)}, u32[]{:S(2)}) collective-permute-start(f32[512,256]{1,0:T(8,128)S(1)} %shard_map.55), channel_id=1, source_target_pairs={{16,0},{17,1},{18,2},{19,3},{20,4},{21,5},{22,6},{23,7},{24,8},{25... | collective-permute-start | bytes 1572872 | tf_op jit(solution)/shard_map/ppermute | solution.py:214
  144.0 135.4 %all-gather.11.cloned.1.call-start = ((), (), s32[]{:S(2)}) async-start(), calls=%async_computation.2 | async-start | bytes 4456448 | tf_op jit(solution)/shard_map/all_gather | solution.py:201
  182.8 27.0 %copy-start.8 = (f32[512,256]{1,0:T(8,128)}, f32[512,256]{1,0:T(8,128)S(1)}, u32[]{:S(2)}) copy-start(f32[512,256]{1,0:T(8,128)S(1)} %get-tuple-element.29.refs_5_) | copy-start | bytes 1572868
  182.8 2.4 copy-start.5
  211.3 15.5 %collective-permute-start.2 = (f32[512,256]{1,0:T(8,128)}, f32[512,256]{1,0:T(8,128)}, u32[]{:S(2)}, u32[]{:S(2)}) collective-permute-start(f32[512,256]{1,0:T(8,128)} %get-tuple-element.32), channel_id=1, source_target_pairs={{16,0},{17,1},{18,2},{19,3},{20,4},{21,5},{22,6},{23,7},{24,8},{25... | collective-permute-start | bytes 1572872 | tf_op jit(solution)/shard_map/ppermute | solution.py:224
  226.9 2.2 copy-start.1
  230.1 16.4 %copy-start.9 = (f32[512,256]{1,0:T(8,128)S(1)}, f32[512,256]{1,0:T(8,128)}, u32[]{:S(2)}) copy-start(f32[512,256]{1,0:T(8,128)} %copy-done.8) | copy-start | bytes 1572868
  245.1 85.5 %all-gather.13.cloned.1.call-start = ((), (), s32[]{:S(2)}) async-start(), calls=%async_computation.3 | async-start | bytes 4456448 | tf_op jit(solution)/shard_map/all_gather | solution.py:201
  245.2 24.3 %collective-permute-start.3 = (f32[512,256]{1,0:T(8,128)}, f32[512,256]{1,0:T(8,128)S(1)}, u32[]{:S(2)}, u32[]{:S(2)}) collective-permute-start(f32[512,256]{1,0:T(8,128)} %copy-done.20), channel_id=1, source_target_pairs={{16,0},{17,1},{18,2},{19,3},{20,4},{21,5},{22,6},{23,7},{24,8},{25... | collective-permute-start | bytes 1572872 | tf_op jit(solution)/shard_map/ppermute | solution.py:237
  247.8 2.2 copy-start.2
  279.4 2.2 copy-start.3
  298.5 51.9 %collective-permute-start.4 = (bf16[3,512,256]{2,1,0:T(8,128)(2,1)}, bf16[3,512,256]{2,1,0:T(8,128)(2,1)}, u32[]{:S(2)}, u32[]{:S(2)}) collective-permute-start(bf16[3,512,256]{2,1,0:T(8,128)(2,1)} %pad_maximum_fusion.1), channel_id=1, source_target_pairs={{0,16},{1,17},{2,18},{3,19},{4,20},{5,21},{6,22},{7,23},{8,24},{9,... | collective-permute-start | bytes 2359304 | tf_op jit(solution)/shard_map/ppermute | solution.py:242
  302.7 16.4 %collective-permute-start.5 = (f32[512,256]{1,0:T(8,128)}, f32[512,256]{1,0:T(8,128)S(1)}, u32[]{:S(2)}, u32[]{:S(2)}) collective-permute-start(f32[512,256]{1,0:T(8,128)} %copy-done.21), channel_id=1, source_target_pairs={{16,0},{17,1},{18,2},{19,3},{20,4},{21,5},{22,6},{23,7},{24,8},{25... | collective-permute-start | bytes 1572872 | tf_op jit(solution)/shard_map/ppermute | solution.py:237
  304.0 2.2 copy-start.4
  330.7 2.2 copy-start.6
  333.9 16.5 %copy-start.22 = (bf16[512,256]{1,0:T(8,128)(2,1)S(1)}, bf16[512,256]{1,0:T(8,128)(2,1)}, u32[]{:S(2)}) copy-start(bf16[512,256]{1,0:T(8,128)(2,1)} %get-tuple-element.46) | copy-start | bytes 786436
  347.0 9.3 %collective-permute-start.6 = (bf16[512,256]{1,0:T(8,128)(2,1)S(1)}, bf16[512,256]{1,0:T(8,128)(2,1)S(1)}, u32[]{:S(2)}, u32[]{:S(2)}) collective-permute-start(bf16[512,256]{1,0:T(8,128)(2,1)S(1)} %get-tuple-element.44), channel_id=1, source_target_pairs={{0,16},{1,17},{2,18},{3,19},{4,20},{5,21},{6,22},{7,23},{8,24},{9,... | collective-permute-start | bytes 786440 | tf_op jit(solution)/shard_map/ppermute | solution.py:243
  (13 other events, 11.6 us)
Sparse Core Ops, SparseCore 0:
  8.9 91.7 all-gather.6
  126.1 34.9 all-gather.14
  162.7 34.0 all-gather.8
  245.2 34.1 all-gather.10
  296.6 34.0 all-gather.12

commit v2 on v0

--- a/solution.py
+++ b/solution.py
@@ -1,14 +1,321 @@
+import functools
+
 import jax
 import jax.numpy as jnp
 from jax import lax
+from jax.experimental import pallas as pl
+from jax.experimental.pallas import tpu as pltpu
 from jax.sharding import PartitionSpec as P
+
+VMEM_LIMIT = 60 * 1024 * 1024
 
 
 def load_update(drive, admit_col, satur_col):
     return (admit_col * drive / jnp.sqrt(1.0 + (satur_col * drive) ** 2)).astype(jnp.bfloat16)
 
 
-def body(lag_matrices, history, excitation, admittance, saturation):
+def ring_of(pairs):
+    order = list(range(pairs))
+    return order[0::2] + order[1::2][::-1]
+
+
+def place_in_ring(pair, pairs):
+    up, across = pair // 2, pair % 2
+    return up + across * (pairs - 1 - 2 * up)
+
+
+def dot(a, b):
+    return jnp.dot(a, b, preferred_element_type=jnp.float32)
+
+
+def call(kernel, name, products, z_blocks, y_blocks, depth, **kwargs):
+    rows, columns, unknowns = name
+    return pl.pallas_call(
+        kernel,
+        compiler_params=pltpu.CompilerParams(vmem_limit_bytes=VMEM_LIMIT),
+        cost_estimate=pl.CostEstimate(
+            flops=2 * products * rows * unknowns * columns,
+            bytes_accessed=2 * unknowns * (z_blocks * rows + y_blocks * columns),
+            transcendentals=0,
+        ),
+        **kwargs,
+    )
+
+
+def add_to(out_ref, total):
+    @pl.when(pl.program_id(0) == 0)
+    def _():
+        out_ref[...] = total
+
+    @pl.when(pl.program_id(0) > 0)
+    def _():
+        out_ref[...] += total
+
+
+def sizes(z, y):
+    return z.shape[1], y.shape[-1], z.shape[2]
+
+
+def whole(rows, columns):
+    return pl.BlockSpec((rows, columns), lambda k: (0, 0))
+
+
+def slots_kernel(count, *refs):
+    z_refs, h_ref, out_ref = refs[:count], refs[count], refs[count + 1]
+    total = dot(z_refs[0][0], h_ref[0])
+    for slot in range(1, count):
+        total += dot(z_refs[slot][0], h_ref[slot])
+    add_to(out_ref, total)
+
+
+def slots_product(pairs, z, h, shift):
+    rows, columns, unknowns = shape = sizes(z, h)
+    depth, count = unknowns // pairs, z.shape[0] - shift
+    return call(
+        functools.partial(slots_kernel, count), shape, count, count, count, depth,
+        grid=(pairs,),
+        in_specs=[
+            pl.BlockSpec((1, rows, depth), lambda k, slot=slot: (slot, 0, k))
+            for slot in range(shift, shift + count)
+        ]
+        + [pl.BlockSpec((count, depth, columns), lambda k: (0, place_in_ring(k, pairs), 0))],
+        out_specs=whole(rows, columns),
+        out_shape=jax.ShapeDtypeStruct((rows, columns), jnp.float32),
+    )(*([z] * count), h)
+
+
+def later_kernel(rows, count, steps, flag_ref, *refs):
+    z_refs, h_ref, now_ref, more_ref = refs[:count], refs[count], refs[count + 1], refs[count + 2]
+    outs, sums = refs[count + 3 : -1], refs[-1]
+    k = pl.program_id(0)
+    later = steps - 2
+
+    @pl.when(k == 0)
+    def _():
+        sums[...] = more_ref[...]
+
+    for slot in range(count):
+        shifts = min(later, count - slot)
+        stack = [z_refs[slot + shift][0] for shift in range(shifts)]
+        stack = stack[0] if shifts == 1 else jnp.concatenate(stack, axis=0)
+        sums[: shifts * rows] += dot(stack, h_ref[slot])
+
+    @pl.when(k == pl.num_programs(0) - 1)
+    def _():
+        first = flag_ref[0] != 0
+        for index, out_ref in enumerate(outs):
+            ahead = min(index, later - 1)
+            theirs = sums[ahead * rows : (ahead + 1) * rows]
+            ours = now_ref[...] if index == 0 else sums[(index - 1) * rows : index * rows]
+            out_ref[...] = jnp.where(first, ours, theirs)
+
+
+def later_products(pairs, flag, z, h, steps, now, more):
+    rows, columns, unknowns = shape = sizes(z, h)
+    depth, count, later = unknowns // pairs, z.shape[0] - 2, steps - 2
+    products = sum(min(later, count - slot) for slot in range(count))
+    return call(
+        functools.partial(later_kernel, rows, count, steps), shape, products, count, count, depth,
+        grid=(pairs,),
+        in_specs=[pl.BlockSpec(memory_space=pltpu.SMEM)]
+        + [
+            pl.BlockSpec((1, rows, depth), lambda k, slot=slot: (slot, 0, k))
+            for slot in range(2, 2 + count)
+        ]
+        + [
+            pl.BlockSpec((count, depth, columns), lambda k: (0, place_in_ring(k, pairs), 0)),
+            whole(rows, columns),
+            whole(later * rows, columns),
+        ],
+        out_specs=[whole(rows, columns)] * (steps - 1),
+        out_shape=[jax.ShapeDtypeStruct((rows, columns), jnp.float32)] * (steps - 1),
+        scratch_shapes=[pltpu.VMEM((later * rows, columns), jnp.float32)],
+    )(flag, *([z] * count), h, now, more)
+
+
+def ahead_kernel(rows, count, *refs):
+    z_refs, y_ref, now_ref, now_out, more_out = (
+        refs[:count], refs[count], refs[count + 1], refs[count + 2], refs[count + 3]
+    )
+    total = dot(jnp.concatenate([z_ref[0] for z_ref in z_refs], axis=0), y_ref[...])
+    add_to(more_out, total[rows:])
+
+    @pl.when(pl.program_id(0) == 0)
+    def _():
+        now_out[...] = now_ref[...] + total[:rows]
+
+    @pl.when(pl.program_id(0) > 0)
+    def _():
+        now_out[...] += total[:rows]
+
+
+def ahead_products(pairs, z, y, now, count):
+    rows, columns, unknowns = shape = sizes(z, y)
+    depth = unknowns // pairs
+    return call(
+        functools.partial(ahead_kernel, rows, count), shape, count, count, 1, depth,
+        grid=(pairs,),
+        in_specs=[
+            pl.BlockSpec((1, rows, depth), lambda k, slot=slot: (slot, 0, k))
+            for slot in range(count)
+        ]
+        + [
+            pl.BlockSpec((depth, columns), lambda k: (place_in_ring(k, pairs), 0)),
+            whole(rows, columns),
+        ],
+        out_specs=[whole(rows, columns), whole((count - 1) * rows, columns)],
+        out_shape=[
+            jax.ShapeDtypeStruct((rows, columns), jnp.float32),
+            jax.ShapeDtypeStruct(((count - 1) * rows, columns), jnp.float32),
+        ],
+    )(*([z] * count), y, now)
+
+
+def spread_kernel(rows, count, *refs):
+    z_refs, y_ref = refs[:count], refs[count]
+    accs, outs = refs[count + 1 : 2 * count + 1], refs[2 * count + 1 :]
+    stack = [z_ref[0] for z_ref in z_refs]
+    total = dot(stack[0] if count == 1 else jnp.concatenate(stack, axis=0), y_ref[...])
+    for index in range(count):
+        term = total[index * rows : (index + 1) * rows]
+
+        @pl.when(pl.program_id(0) == 0)
+        def _():
+            outs[index][...] = accs[index][...] + term
+
+        @pl.when(pl.program_id(0) > 0)
+        def _():
+            outs[index][...] += term
+
+
+def spread(pairs, z, y, accs):
+    rows, columns, unknowns = shape = sizes(z, y)
+    depth, count = unknowns // pairs, len(accs)
+    return call(
+        functools.partial(spread_kernel, rows, count), shape, count, count, 1, depth,
+        grid=(pairs,),
+        in_specs=[
+            pl.BlockSpec((1, rows, depth), lambda k, slot=slot: (slot, 0, k))
+            for slot in range(1, 1 + count)
+        ]
+        + [pl.BlockSpec((depth, columns), lambda k: (place_in_ring(k, pairs), 0))]
+        + [whole(rows, columns)] * count,
+        out_specs=[whole(rows, columns)] * count,
+        out_shape=[jax.ShapeDtypeStruct((rows, columns), jnp.float32)] * count,
+    )(*([z] * count), y, *accs)
+
+
+def step_kernel(
+    pairs, flag_ref, z_ref, y_ref, base_ref, next_ref, admit_ref, satur_ref, drive_ref, send_ref,
+    z_buf, y_buf, base_buf, next_buf, z_sems, y_sems, sems,
+):
+    depth = z_buf.shape[1] // pairs
+    copies = []
+    for at, pair in enumerate(ring_of(pairs)):
+        across, down = pl.ds(pair * depth, depth), pl.ds(at * depth, depth)
+        copies.append((
+            pltpu.make_async_copy(z_ref.at[0, :, across], z_buf.at[:, across], z_sems.at[at]),
+            pltpu.make_async_copy(y_ref.at[down, :], y_buf.at[down, :], y_sems.at[at]),
+        ))
+    for z_copy, y_copy in copies:
+        z_copy.start()
+        y_copy.start()
+    base_copy = pltpu.make_async_copy(base_ref, base_buf, sems.at[0])
+    next_copy = pltpu.make_async_copy(next_ref, next_buf, sems.at[1])
+    base_copy.start()
+    next_copy.start()
+    for at, pair in enumerate(ring_of(pairs)):
+        for copy in copies[at]:
+            copy.wait()
+        term = dot(z_buf[:, pair * depth : (pair + 1) * depth], y_buf[at * depth : (at + 1) * depth])
+        if at == 0:
+            drive_ref[...] = term
+        else:
+            drive_ref[...] += term
+    base_copy.wait()
+    next_copy.wait()
+    drive = base_buf[...] - drive_ref[...]
+    drive_ref[...] = drive
+    density = load_update(drive, admit_ref[...], satur_ref[...])
+    send_ref[...] = jnp.where(flag_ref[0] != 0, density, next_buf[...])
+
+
+def step(pairs, flag, z, y, base, following, admit_col, satur_col):
+    rows, columns, unknowns = shape = sizes(z, y)
+    vmem, hbm = pl.BlockSpec(memory_space=pltpu.VMEM), pl.BlockSpec(memory_space=pl.ANY)
+    return call(
+        functools.partial(step_kernel, pairs), shape, 1, 1, 1, unknowns // pairs,
+        in_specs=[pl.BlockSpec(memory_space=pltpu.SMEM), hbm, hbm, hbm, hbm, vmem, vmem],
+        out_specs=[vmem, vmem],
+        out_shape=[
+            jax.ShapeDtypeStruct((rows, columns), jnp.float32),
+            jax.ShapeDtypeStruct((rows, columns), jnp.bfloat16),
+        ],
+        scratch_shapes=[
+            pltpu.VMEM((rows, unknowns), jnp.bfloat16),
+            pltpu.VMEM((unknowns, columns), jnp.bfloat16),
+            pltpu.VMEM((rows, columns), jnp.float32),
+            pltpu.VMEM((rows, columns), jnp.bfloat16),
+            pltpu.SemaphoreType.DMA((pairs,)),
+            pltpu.SemaphoreType.DMA((pairs,)),
+            pltpu.SemaphoreType.DMA((2,)),
+        ],
+    )(flag, z, y, base, following, admit_col, satur_col)
+
+
+def gather_rows(pairs, block, axis):
+    order = [2 * pair + core for pair in ring_of(pairs) for core in (0, 1)]
+    return lax.all_gather(block, "row", axis=axis, tiled=True, axis_index_groups=[order])
+
+
+def two_group_body(pairs, lag_matrices, history, excitation, admittance, saturation):
+    z, steps = lag_matrices, excitation.shape[0]
+    slots = z.shape[0]
+    is_first = lax.axis_index("lag") == 0
+    flag = is_first.astype(jnp.int32)[None]
+    admit_col, satur_col = admittance[:, None], saturation[:, None]
+    down, up = [(1, 0)], [(0, 1)]
+
+    incoming = lax.ppermute(history[slots - (steps - 1) :], "lag", up)
+    archive = gather_rows(pairs, history, 1)
+    archive, incoming = lax.optimization_barrier((archive, incoming))
+    ahead = gather_rows(pairs, incoming[steps - 2], 0)
+
+    first_part = slots_product(pairs, z, archive, 0)
+    first_other = lax.ppermute(first_part, "lag", down)
+    archive, first_part = lax.optimization_barrier((archive, first_part))
+    now = slots_product(pairs, z, archive, 1)
+    now, first_part = lax.optimization_barrier((now, first_part))
+    density = load_update(excitation[0] - (first_part + first_other), admit_col, satur_col)
+    send = jnp.where(is_first, density, incoming[steps - 3])
+    results = [send]
+    fresh = gather_rows(pairs, send, 0)
+
+    ahead, send = lax.optimization_barrier((ahead, send))
+    now, more = ahead_products(pairs, z, ahead, now, steps - 1)
+    other = lax.ppermute(-now, "lag", down)
+    archive, now, more = lax.optimization_barrier((archive, now, more))
+    accs = later_products(pairs, flag, z, archive, steps, now, more)
+
+    for index in range(1, steps):
+        base = jnp.where(is_first, excitation[index] + other, 0.0) - accs[0]
+        following = incoming[max(steps - 3 - index, 0)]
+        drive, send = step(pairs, flag, z, fresh, base, following, admit_col, satur_col)
+        results.append(send)
+        if index + 1 < steps:
+            rows_before = fresh
+            fresh = gather_rows(pairs, send, 0)
+            other = lax.ppermute(drive, "lag", down)
+            rows_before, send = lax.optimization_barrier((rows_before, send))
+            accs = spread(pairs, z, rows_before, accs[1:])
+
+    early = jnp.stack(results[:-1])
+    early = jnp.where(is_first, early, lax.ppermute(early, "lag", up))
+    last = jnp.where(is_first, results[-1], lax.ppermute(results[-1], "lag", up))
+    return jnp.concatenate([early, last[None]], axis=0)
+
+
+def general_body(lag_matrices, history, excitation, admittance, saturation):
     slot_count = lag_matrices.shape[0]
     step_count = excitation.shape[0]
     lag_index = lax.axis_index("lag")
@@ -32,6 +339,7 @@
 
 
 def solution(mesh):
+    groups, members = mesh.shape["lag"], mesh.shape["row"]
     placed = (
         P("lag", "row", None),
         P("lag", "row", None),
@@ -39,6 +347,15 @@
         P("row"),
         P("row"),
     )
+
+    def body(lag_matrices, history, excitation, admittance, saturation):
+        slots, steps = lag_matrices.shape[0], excitation.shape[0]
+        chosen = general_body
+        depth = lag_matrices.shape[2] // members
+        if groups == 2 and members % 4 == 0 and depth % 128 == 0 and 2 < steps <= slots:
+            chosen = functools.partial(two_group_body, members // 2)
+        return chosen(lag_matrices, history, excitation, admittance, saturation)
+
     return jax.shard_map(
         body, mesh=mesh, in_specs=placed, out_specs=P(None, "row", None), check_vma=False
     )

time: 601 us -> 294 us (0.49)
  waiting for transfers between devices: 433 us -> 129 us
  Pallas kernels: 0 us -> 116 us
  matrix products: 75.9 us -> 0 us
  local copies, waits for them, and re-layouts: 48.7 us -> 3.76 us
  starting transfers between devices: 0.51 us -> 18.7 us
  other arithmetic: 29.8 us -> 11.9 us
    all_gather x5, waiting for transfers between devices: 325 us -> 104 us  [gather_rows(): lax.all_gather(block, 'row', axis=axis, tiled=True, axis_index_groups=[or...]
    pallas_call x0 -> x9, Pallas kernels: none -> 116 us  [the longest x2 37.2 us: slots_product(): call(functools.partial(slots_kernel, count), shape, count, count, count,...]
    psum x4 -> x0, waiting for transfers between devices: 106 us -> none  [body(): summed = lax.psum(partial_sum, 'lag')]
    dot_general x4 -> x0, matrix products: 75.9 us -> none  [body(): jnp.einsum('lrm,lmc->rc', lag_matrices, own_slots, preferred_element_type...]
    slice x3 -> x1, local copies, waits for them, and re-layouts: 41.6 us -> 1.19 us  [two_group_body(): incoming = lax.ppermute(history[slots - (steps - 1):], 'lag', up)]
    ppermute x0 -> x7, waiting for transfers between devices: none -> 24.5 us  [the longest x1 16.7 us: two_group_body(): incoming = lax.ppermute(history[slots - (steps - 1):], 'lag', up)]
    concatenate x1, other arithmetic: 22.8 us -> 1.06 us  [two_group_body(): return jnp.concatenate([early, last[None]], axis=0)]
    ppermute x0 -> x7, starting transfers between devices: none -> 18.5 us  [the longest x1 4.92 us: two_group_body(): incoming = lax.ppermute(history[slots - (steps - 1):], 'lag', up)]
  transfers between devices with their start and end apart: 9 -> 12, of which waited for: 9 -> 6; matrix products, arithmetic and copies ran while one was open for 7% -> 4% of each run, Pallas kernels for 0% -> 34%
where the time goes in v2:
time: 294 us; the launch traced here: 293 us
  waiting for transfers between devices  129 us (44%)
  Pallas kernels  116 us (39%)
  starting transfers between devices  18.7 us (6%)
  between operations  13.3 us (5%)
  other arithmetic  11.9 us (4%)
  local copies, waits for them, and re-layouts  3.76 us (1%)
    all_gather x5, waiting for transfers between devices, gather_rows(): lax.all_gather(block, 'row', axis=axis, tiled=True, axis_index_groups=[or...  104 us
    pallas_call x2, Pallas kernels, slots_product(): call(functools.partial(slots_kernel, count), shape, count, count, count,...  37.2 us
    pallas_call x3, Pallas kernels, step(): call(functools.partial(step_kernel, pairs), shape, 1, 1, 1, unknowns // p...  25.5 us
    pallas_call x2, Pallas kernels, spread(): call(functools.partial(spread_kernel, rows, count), shape, count, count,...  22.6 us
    ppermute x1, waiting for transfers between devices, two_group_body(): incoming = lax.ppermute(history[slots - (steps - 1):], 'lag', up)  16.7 us
    pallas_call x1, Pallas kernels, ahead_products(): call(functools.partial(ahead_kernel, rows, count), shape, count, count, 1...  16 us
    pallas_call x1, Pallas kernels, later_products(): call(functools.partial(later_kernel, rows, count, steps), shape, products...  15.2 us
    ppermute x1, waiting for transfers between devices, two_group_body(): lax.ppermute(results[-1], 'lag', up)  6.11 us
  transfers between devices with their start and end apart: 12, of which 6 were waited for; matrix products, arithmetic and copies ran while one was open for 4% of the time, Pallas kernels for 34%

profile of v2, /device:TPU:0, one launch (start us, length us, event | category | flops | bytes accessed | tf_op | source)
XLA Modules:
  0.0 293.0 jit_solution(9973459103322746611)
XLA Ops:
  8.5 4.9 %collective-permute-start = (bf16[3,512,256]{2,1,0:T(8,128)(2,1)S(1)}, bf16[3,512,256]{2,1,0:T(8,128)(2,1)S(1)}, u32[]{:S(2)}, u32[]{:S(2)}) collective-permute-start(bf16[3,512,256]{2,1,0:T(8,128)(2,1)S(1)} %slice.27), channel_id=1, source_target_pairs={{0,16},{1,17},{2,18},{3,19},{4,20},{5,21},{6,22},{7,23},{8,24},{9,... | collective-permute-start | bytes 2359304 | tf_op jit(solution)/shard_map/ppermute | solution.py:279
  13.4 16.7 %collective-permute-done = bf16[3,512,256]{2,1,0:T(8,128)(2,1)S(1)} collective-permute-done((bf16[3,512,256]{2,1,0:T(8,128)(2,1)S(1)}, bf16[3,512,256]{2,1,0:T(8,128)(2,1)S(1)}, u32[]{:S(2)}, u32[]{:S(2)}) %collective-permute-start) | collective-permute-done | bytes 786464 | tf_op jit(solution)/shard_map/ppermute | solution.py:279
  30.2 70.6 %all-gather.7.cloned.1.call-done.refs_4_.refs_3_.refs_2_ = bf16[4,8192,256]{2,1,0:T(8,128)(2,1)} async-done(((bf16[4,512,256]{2,1,0:T(8,128)(2,1)}), bf16[4,8192,256]{2,1,0:T(8,128)(2,1)}) %all-gather.7.cloned.1.call-update) | async-done | bytes 16777232 | tf_op jit(solution)/shard_map/all_gather | solution.py:268
  101.6 20.4 %shard_map.55 = f32[512,256]{1,0:T(8,128)} custom-call(bf16[4,512,8192]{2,1,0:T(8,128)(2,1)} %z_ref.5, bf16[4,512,8192]{2,1,0:T(8,128)(2,1)} %z_ref.5, bf16[4,512,8192]{2,1,0:T(8,128)(2,1)} %z_ref.5, bf16[4,512,8192]{2,1,0:T(8,128)(2,1)} %z_ref.5, bf16[4,8192,256]{2,1,0:T(8,128)(2,1)} %all-gather.7.cloned.1.call-done.refs_4_.refs_3_.refs_2_), custom_call_target="tpu_custom_call" | custom-call | flops 8589934592 | bytes 50331648 | tf_op jit(solution)/shard_map/pallas_call | solution.py:74
  122.0 1.6 collective-permute-start.1
  123.6 16.9 %shard_map.56.refs_4_ = f32[512,256]{1,0:T(8,128)} custom-call(bf16[4,512,8192]{2,1,0:T(8,128)(2,1)} %z_ref.5, bf16[4,512,8192]{2,1,0:T(8,128)(2,1)} %z_ref.5, bf16[4,512,8192]{2,1,0:T(8,128)(2,1)} %z_ref.5, bf16[4,8192,256]{2,1,0:T(8,128)(2,1)} %all-gather.7.cloned.1.call-done.refs_4_.refs_3_.refs_2_), custom_call_target="tpu_custom_call" | custom-call | flops 6442450944 | bytes 37748736 | tf_op jit(solution)/shard_map/pallas_call | solution.py:74
  143.2 16.0 %shard_map.57 = (f32[512,256]{1,0:T(8,128)}, f32[1024,256]{1,0:T(8,128)}) custom-call(bf16[4,512,8192]{2,1,0:T(8,128)(2,1)} %z_ref.5, bf16[4,512,8192]{2,1,0:T(8,128)(2,1)} %z_ref.5, bf16[4,512,8192]{2,1,0:T(8,128)(2,1)} %z_ref.5, bf16[8192,256]{1,0:T(8,128)(2,1)} %bitcast.37, f32[512,256]{1,0:T(8,128)} %shard_map.56.refs_4_), custom_call_target="tpu_custom_call" | custom-call | flops 6442450944 | bytes 29360128 | tf_op jit(solution)/shard_map/pallas_call | solution.py:155
  161.6 15.2 %shard_map.58 = (f32[512,256]{1,0:T(8,128)}, f32[512,256]{1,0:T(8,128)}, f32[512,256]{1,0:T(8,128)}) custom-call(s32[1]{0:T(128)} %bitcast.3.flag_ref, bf16[4,512,8192]{2,1,0:T(8,128)(2,1)} %z_ref.5, bf16[4,512,8192]{2,1,0:T(8,128)(2,1)} %z_ref.5, bf16[4,8192,256]{2,1,0:T(8,128)(2,1)} %all-gather.7.cloned.1.call-done.refs_4_.refs_3_.refs_2_, ...), custom_call_target="tpu_custom_call" | custom-call | flops 6442450944 | bytes 25165824 | tf_op jit(solution)/shard_map/pallas_call | solution.py:117
  176.8 1.9 fusion.5.base_ref
  178.7 8.5 %shard_map.59 = (f32[512,256]{1,0:T(8,128)}, bf16[512,256]{1,0:T(8,128)(2,1)}) custom-call(s32[1]{0:T(128)} %bitcast.3.flag_ref, bf16[4,512,8192]{2,1,0:T(8,128)(2,1)} %z_ref.5, bf16[8192,256]{1,0:T(8,128)(2,1)} %all-gather.9.cloned.1.call-done.y_ref.refs_2_, f32[512,256]{1,0:T(8,128)} %fusion.5.base_ref, bf16[512,256]{1,0:T(8,128)(2,1)} %get-tuple-element.53.next_ref, ...), custom_call_target="tpu_custom_call" | custom-call | flops 2147483648 | bytes 12582912 | tf_op jit(solution)/shard_map/pallas_call | solution.py:246
  188.6 13.2 %shard_map.60 = (f32[512,256]{1,0:T(8,128)}, f32[512,256]{1,0:T(8,128)}) custom-call(bf16[4,512,8192]{2,1,0:T(8,128)(2,1)} %z_ref.5, bf16[4,512,8192]{2,1,0:T(8,128)(2,1)} %z_ref.5, bf16[8192,256]{1,0:T(8,128)(2,1)} %all-gather.9.cloned.1.call-done.y_ref.refs_2_, f32[512,256]{1,0:T(8,128)} %get-tuple-element.45.refs_3_, f32[512,256]{1,0:T(8,128)} %get-tuple-element.46.refs_4_), custom_call_target="tpu_custom_call" | custom-call | flops 4294967296 | bytes 20971520 | tf_op jit(solution)/shard_map/pallas_call | solution.py:194
  201.8 1.6 collective-permute-done.3
  203.4 1.9 fusion.3.base_ref
  205.4 18.2 %all-gather.11.cloned.1.call-done.y_ref.refs_1_ = bf16[8192,256]{1,0:T(8,128)(2,1)} async-done(((bf16[512,256]{1,0:T(8,128)(2,1)}), bf16[8192,256]{1,0:T(8,128)(2,1)}) %all-gather.11.cloned.1.call-update) | async-done | bytes 4194320 | tf_op jit(solution)/shard_map/all_gather | solution.py:268
  223.6 8.5 %shard_map.61 = (f32[512,256]{1,0:T(8,128)}, bf16[512,256]{1,0:T(8,128)(2,1)}) custom-call(s32[1]{0:T(128)} %bitcast.3.flag_ref, bf16[4,512,8192]{2,1,0:T(8,128)(2,1)} %z_ref.5, bf16[8192,256]{1,0:T(8,128)(2,1)} %all-gather.11.cloned.1.call-done.y_ref.refs_1_, f32[512,256]{1,0:T(8,128)} %fusion.3.base_ref, bf16[512,256]{1,0:T(8,128)(2,1)} %get-tuple-element.53.next_ref, ...), custom_call_target="tpu_custom_call" | custom-call | flops 2147483648 | bytes 12582912 | tf_op jit(solution)/shard_map/pallas_call | solution.py:246
  232.1 1.5 collective-permute-start.5
  233.6 1.9 pad_maximum_fusion.1
  235.6 4.6 %collective-permute-start.4 = (bf16[3,512,256]{2,1,0:T(8,128)(2,1)}, bf16[3,512,256]{2,1,0:T(8,128)(2,1)S(1)}, u32[]{:S(2)}, u32[]{:S(2)}) collective-permute-start(bf16[3,512,256]{2,1,0:T(8,128)(2,1)} %pad_maximum_fusion.1), channel_id=1, source_target_pairs={{0,16},{1,17},{2,18},{3,19},{4,20},{5,21},{6,22},{7,23},{8,24},{9,... | collective-permute-start | bytes 2359304 | tf_op jit(solution)/shard_map/ppermute | solution.py:313
  240.2 9.4 %shard_map.62 = f32[512,256]{1,0:T(8,128)} custom-call(bf16[4,512,8192]{2,1,0:T(8,128)(2,1)} %z_ref.5, bf16[8192,256]{1,0:T(8,128)(2,1)} %all-gather.11.cloned.1.call-done.y_ref.refs_1_, f32[512,256]{1,0:T(8,128)} %get-tuple-element.51.refs_2_), custom_call_target="tpu_custom_call" | custom-call | flops 2147483648 | bytes 12582912 | tf_op jit(solution)/shard_map/pallas_call | solution.py:194
  249.6 1.9 fusion.1.base_ref
  251.5 14.8 %all-gather.13.cloned.1.call-done.y_ref = bf16[8192,256]{1,0:T(8,128)(2,1)} async-done(((bf16[512,256]{1,0:T(8,128)(2,1)}), bf16[8192,256]{1,0:T(8,128)(2,1)}) %all-gather.13.cloned.1.call-update) | async-done | bytes 4194320 | tf_op jit(solution)/shard_map/all_gather | solution.py:268
  266.3 8.5 %shard_map.63 = (f32[512,256]{1,0:T(8,128)}, bf16[512,256]{1,0:T(8,128)(2,1)}) custom-call(s32[1]{0:T(128)} %bitcast.3.flag_ref, bf16[4,512,8192]{2,1,0:T(8,128)(2,1)} %z_ref.5, bf16[8192,256]{1,0:T(8,128)(2,1)} %all-gather.13.cloned.1.call-done.y_ref, f32[512,256]{1,0:T(8,128)} %fusion.1.base_ref, bf16[512,256]{1,0:T(8,128)(2,1)} %get-tuple-element.53.next_ref, ...), custom_call_target="tpu_custom_call" | custom-call | flops 2147483648 | bytes 12582912 | tf_op jit(solution)/shard_map/pallas_call | solution.py:246
  274.8 3.4 %collective-permute-start.6 = (bf16[512,256]{1,0:T(8,128)(2,1)}, bf16[512,256]{1,0:T(8,128)(2,1)S(1)}, u32[]{:S(2)}, u32[]{:S(2)}) collective-permute-start(bf16[512,256]{1,0:T(8,128)(2,1)} %get-tuple-element.52), channel_id=1, source_target_pairs={{0,16},{1,17},{2,18},{3,19},{4,20},{5,21},{6,22},{7,23},{8,24},{9,... | collective-permute-start | bytes 786440 | tf_op jit(solution)/shard_map/ppermute | solution.py:314
  278.4 6.1 %collective-permute-done.6 = bf16[512,256]{1,0:T(8,128)(2,1)S(1)} collective-permute-done((bf16[512,256]{1,0:T(8,128)(2,1)}, bf16[512,256]{1,0:T(8,128)(2,1)S(1)}, u32[]{:S(2)}, u32[]{:S(2)}) %collective-permute-start.6) | collective-permute-done | bytes 262176 | tf_op jit(solution)/shard_map/ppermute | solution.py:314
  (41 shorter events, 11.5 us)
Async XLA Ops:
  6.5 94.2 %all-gather.7.cloned.1.call-start = ((), (), s32[]{:S(2)}) async-start(), calls=%async_computation | async-start | bytes 17825792 | tf_op jit(solution)/shard_map/all_gather | solution.py:268
  7.3 136.0 %all-gather.15.cloned.1.call-start = ((), (), s32[]{:S(2)}) async-start(), calls=%async_computation.4 | async-start | bytes 4456448 | tf_op jit(solution)/shard_map/all_gather | solution.py:268
  8.5 21.7 %collective-permute-start = (bf16[3,512,256]{2,1,0:T(8,128)(2,1)S(1)}, bf16[3,512,256]{2,1,0:T(8,128)(2,1)S(1)}, u32[]{:S(2)}, u32[]{:S(2)}) collective-permute-start(bf16[3,512,256]{2,1,0:T(8,128)(2,1)S(1)} %slice.27), channel_id=1, source_target_pairs={{0,16},{1,17},{2,18},{3,19},{4,20},{5,21},{6,22},{7,23},{8,24},{9,... | collective-permute-start | bytes 2359304 | tf_op jit(solution)/shard_map/ppermute | solution.py:279
  101.6 77.2 %all-gather.9.cloned.1.call-start = ((), (), s32[]{:S(2)}) async-start(), calls=%async_computation.1 | async-start | bytes 4456448 | tf_op jit(solution)/shard_map/all_gather | solution.py:268
  122.0 18.4 %copy-start.3 = (f32[512,256]{1,0:T(8,128)S(1)}, f32[512,256]{1,0:T(8,128)}, u32[]{:S(2)}) copy-start(f32[512,256]{1,0:T(8,128)} %shard_map.55) | copy-start | bytes 1572868
  122.0 18.4 %copy-start.4 = (f32[4,512,256]{2,1,0:T(8,128)S(1)}, f32[4,512,256]{2,1,0:T(8,128)}, u32[]{:S(2)}) copy-start(f32[4,512,256]{2,1,0:T(8,128)} %param.7) | copy-start | bytes 6291460
  122.0 18.5 %copy-start.5 = (f32[512]{0:T(512)S(1)}, f32[512]{0:T(512)}, u32[]{:S(2)}) copy-start(f32[512]{0:T(512)} %param.8) | copy-start | bytes 6148
  122.0 18.5 %copy-start.6 = (f32[512]{0:T(512)S(1)}, f32[512]{0:T(512)}, u32[]{:S(2)}) copy-start(f32[512]{0:T(512)} %param.9) | copy-start | bytes 6148
  122.0 18.4 %collective-permute-start.1 = (f32[512,256]{1,0:T(8,128)}, f32[512,256]{1,0:T(8,128)S(1)}, u32[]{:S(2)}, u32[]{:S(2)}) collective-permute-start(f32[512,256]{1,0:T(8,128)} %shard_map.55), channel_id=1, source_target_pairs={{16,0},{17,1},{18,2},{19,3},{20,4},{21,5},{22,6},{23,7},{24,8},{25... | collective-permute-start | bytes 1572872 | tf_op jit(solution)/shard_map/ppermute | solution.py:285
  141.4 82.2 %all-gather.11.cloned.1.call-start = ((), (), s32[]{:S(2)}) async-start(), calls=%async_computation.2 | async-start | bytes 4456448 | tf_op jit(solution)/shard_map/all_gather | solution.py:268
  160.3 16.5 %collective-permute-start.2 = (f32[512,256]{1,0:T(8,128)S(1)}, f32[512,256]{1,0:T(8,128)S(1)}, u32[]{:S(2)}, u32[]{:S(2)}) collective-permute-start(f32[512,256]{1,0:T(8,128)S(1)} %neg.3), channel_id=1, source_target_pairs={{16,0},{17,1},{18,2},{19,3},{20,4},{21,5},{22,6},{23,7},{24,8},{25... | collective-permute-start | bytes 1572872 | tf_op jit(solution)/shard_map/ppermute | solution.py:296
  187.3 79.1 %all-gather.13.cloned.1.call-start = ((), (), s32[]{:S(2)}) async-start(), calls=%async_computation.3 | async-start | bytes 4456448 | tf_op jit(solution)/shard_map/all_gather | solution.py:268
  187.3 16.1 %collective-permute-start.3 = (f32[512,256]{1,0:T(8,128)}, f32[512,256]{1,0:T(8,128)S(1)}, u32[]{:S(2)}, u32[]{:S(2)}) collective-permute-start(f32[512,256]{1,0:T(8,128)} %get-tuple-element.43), channel_id=1, source_target_pairs={{16,0},{17,1},{18,2},{19,3},{20,4},{21,5},{22,6},{23,7},{24,8},{25... | collective-permute-start | bytes 1572872 | tf_op jit(solution)/shard_map/ppermute | solution.py:308
  205.4 28.2 %copy-start = (bf16[512,256]{1,0:T(8,128)(2,1)S(1)}, bf16[512,256]{1,0:T(8,128)(2,1)}, u32[]{:S(2)}) copy-start(bf16[512,256]{1,0:T(8,128)(2,1)} %fusion.6) | copy-start | bytes 786436
  205.4 28.2 %copy-start.1 = (bf16[512,256]{1,0:T(8,128)(2,1)S(1)}, bf16[512,256]{1,0:T(8,128)(2,1)}, u32[]{:S(2)}) copy-start(bf16[512,256]{1,0:T(8,128)(2,1)} %get-tuple-element.42) | copy-start | bytes 786436
  232.1 17.4 %collective-permute-start.5 = (f32[512,256]{1,0:T(8,128)}, f32[512,256]{1,0:T(8,128)S(1)}, u32[]{:S(2)}, u32[]{:S(2)}) collective-permute-start(f32[512,256]{1,0:T(8,128)} %get-tuple-element.49), channel_id=1, source_target_pairs={{16,0},{17,1},{18,2},{19,3},{20,4},{21,5},{22,6},{23,7},{24,8},{25... | collective-permute-start | bytes 1572872 | tf_op jit(solution)/shard_map/ppermute | solution.py:308
  235.6 42.7 %collective-permute-start.4 = (bf16[3,512,256]{2,1,0:T(8,128)(2,1)}, bf16[3,512,256]{2,1,0:T(8,128)(2,1)S(1)}, u32[]{:S(2)}, u32[]{:S(2)}) collective-permute-start(bf16[3,512,256]{2,1,0:T(8,128)(2,1)} %pad_maximum_fusion.1), channel_id=1, source_target_pairs={{0,16},{1,17},{2,18},{3,19},{4,20},{5,21},{6,22},{7,23},{8,24},{9,... | collective-permute-start | bytes 2359304 | tf_op jit(solution)/shard_map/ppermute | solution.py:313
  251.5 26.7 %copy-start.2 = (bf16[512,256]{1,0:T(8,128)(2,1)S(1)}, bf16[512,256]{1,0:T(8,128)(2,1)}, u32[]{:S(2)}) copy-start(bf16[512,256]{1,0:T(8,128)(2,1)} %get-tuple-element.48) | copy-start | bytes 786436
  274.8 9.7 %collective-permute-start.6 = (bf16[512,256]{1,0:T(8,128)(2,1)}, bf16[512,256]{1,0:T(8,128)(2,1)S(1)}, u32[]{:S(2)}, u32[]{:S(2)}) collective-permute-start(bf16[512,256]{1,0:T(8,128)(2,1)} %get-tuple-element.52), channel_id=1, source_target_pairs={{0,16},{1,17},{2,18},{3,19},{4,20},{5,21},{6,22},{7,23},{8,24},{9,... | collective-permute-start | bytes 786440 | tf_op jit(solution)/shard_map/ppermute | solution.py:314
Sparse Core Ops, SparseCore 0:
  8.9 91.7 all-gather.6
  102.3 34.9 all-gather.14
  141.6 36.1 all-gather.8
  187.4 36.1 all-gather.10
  232.3 34.0 all-gather.12

commit v3 on v2

v3 whole, which is shorter than its diff:
```python
import functools
import math

import jax
import jax.numpy as jnp
from jax import lax
from jax.experimental import pallas as pl
from jax.experimental.pallas import tpu as pltpu
from jax.sharding import PartitionSpec as P

VMEM_LIMIT = 60 * 1024 * 1024


def load_update(drive, admit_col, satur_col):
    return (admit_col * drive * lax.rsqrt(1.0 + (satur_col * drive) ** 2)).astype(jnp.bfloat16)


def ring_of(pairs):
    order = list(range(pairs))
    return order[0::2] + order[1::2][::-1]


def place_in_ring(pair, pairs):
    up, across = pair // 2, pair % 2
    return up + across * (pairs - 1 - 2 * up)


def dot(a, b):
    return jnp.dot(a, b, preferred_element_type=jnp.float32)


def call(kernel, shape, products, z_blocks, y_blocks, **kwargs):
    rows, columns, unknowns = shape
    return pl.pallas_call(
        kernel,
        compiler_params=pltpu.CompilerParams(vmem_limit_bytes=VMEM_LIMIT),
        cost_estimate=pl.CostEstimate(
            flops=2 * products * rows * unknowns * columns,
            bytes_accessed=2 * unknowns * (z_blocks * rows + y_blocks * columns),
            transcendentals=0,
        ),
        **kwargs,
    )


def add_to(out_ref, total):
    @pl.when(pl.program_id(0) == 0)
    def _():
        out_ref[...] = total

    @pl.when(pl.program_id(0) > 0)
    def _():
        out_ref[...] += total


def sizes(z, y):
    return z.shape[1], y.shape[-1], z.shape[2]


def whole(rows, columns):
    return pl.BlockSpec((rows, columns), lambda k: (0, 0))


def z_spec(rows, depth, slot):
    return pl.BlockSpec((1, rows, depth), lambda k: (slot, 0, k))


def h_spec(depth, columns, first, count, pairs):
    return pl.BlockSpec((count, depth, columns), lambda k: (first, place_in_ring(k, pairs), 0))


def y_spec(depth, columns, pairs):
    return pl.BlockSpec((depth, columns), lambda k: (place_in_ring(k, pairs), 0))


def stacked(z_refs):
    if len(z_refs) == 1:
        return z_refs[0][0]
    return jnp.concatenate([z_ref[0] for z_ref in z_refs], axis=0)


def slots_kernel(count, *refs):
    z_refs, h_ref, out_ref = refs[:count], refs[count], refs[count + 1]
    total = dot(z_refs[0][0], h_ref[0])
    for slot in range(1, count):
        total += dot(z_refs[slot][0], h_ref[slot])
    add_to(out_ref, total)


def slots_product(pairs, z, h, shift, count):
    rows, columns, unknowns = shape = sizes(z, h)
    depth = unknowns // pairs
    return call(
        functools.partial(slots_kernel, count), shape, count, count, count,
        grid=(pairs,),
        in_specs=[z_spec(rows, depth, slot) for slot in range(shift, shift + count)]
        + [h_spec(depth, columns, 0, count, pairs)],
        out_specs=whole(rows, columns),
        out_shape=jax.ShapeDtypeStruct((rows, columns), jnp.float32),
    )(*([z] * count), h)


def next_kernel(z_new_ref, y_ref, z_old_ref, h_ref, part_ref, out_ref):
    total = dot(z_new_ref[0], y_ref[...]) + dot(z_old_ref[0], h_ref[0])

    @pl.when(pl.program_id(0) == 0)
    def _():
        out_ref[...] = -part_ref[...] - total

    @pl.when(pl.program_id(0) > 0)
    def _():
        out_ref[...] -= total


def next_product(pairs, z, y, h, slot, part):
    rows, columns, unknowns = shape = sizes(z, y)
    depth = unknowns // pairs
    return call(
        next_kernel, shape, 2, 2, 2,
        grid=(pairs,),
        in_specs=[
            z_spec(rows, depth, 0),
            y_spec(depth, columns, pairs),
            z_spec(rows, depth, slot + 1),
            h_spec(depth, columns, slot, 1, pairs),
            whole(rows, columns),
        ],
        out_specs=whole(rows, columns),
        out_shape=jax.ShapeDtypeStruct((rows, columns), jnp.float32),
    )(z, y, z, h, part)


def later_kernel(rows, low, high, top, *refs):
    z_refs, y_ref, h_ref, outs, sums = refs[:top], refs[top], refs[top + 1], refs[top + 2 : -1], refs[-1]
    k = pl.program_id(0)

    @pl.when(k == 0)
    def _():
        sums[...] = jnp.zeros_like(sums)

    sums[...] -= dot(stacked(z_refs[: high - low]), y_ref[...])
    for slot in range(h_ref.shape[0]):
        stack = z_refs[slot + 1 : min(slot + 1 + high - low, top)]
        sums[: len(stack) * rows] -= dot(stacked(stack), h_ref[slot])

    @pl.when(k == pl.num_programs(0) - 1)
    def _():
        for index, out_ref in enumerate(outs):
            out_ref[...] = sums[index * rows : (index + 1) * rows]


def later_products(pairs, z, y, h, low, high):
    rows, columns, unknowns = shape = sizes(z, h)
    depth, top = unknowns // pairs, z.shape[0] - 1 - low
    count = max(top - 1, 1)
    products = high - low + sum(min(high - low, top - 1 - slot) for slot in range(top - 1))
    return call(
        functools.partial(later_kernel, rows, low, high, top), shape, products, top, count + 1,
        grid=(pairs,),
        in_specs=[z_spec(rows, depth, slot) for slot in range(low + 1, low + 1 + top)]
        + [y_spec(depth, columns, pairs), h_spec(depth, columns, 0, count, pairs)],
        out_specs=[whole(rows, columns)] * (high - low),
        out_shape=[jax.ShapeDtypeStruct((rows, columns), jnp.float32)] * (high - low),
        scratch_shapes=[pltpu.VMEM(((high - low) * rows, columns), jnp.float32)],
    )(*([z] * top), y, h)


def spread_kernel(rows, count, *refs):
    z_refs, y_ref = refs[:count], refs[count]
    accs, outs = refs[count + 1 : 2 * count + 1], refs[2 * count + 1 :]
    total = dot(stacked(z_refs), y_ref[...])
    for index in range(count):
        term = total[index * rows : (index + 1) * rows]

        @pl.when(pl.program_id(0) == 0)
        def _():
            outs[index][...] = accs[index][...] - term

        @pl.when(pl.program_id(0) > 0)
        def _():
            outs[index][...] -= term


def spread(pairs, z, y, accs):
    rows, columns, unknowns = shape = sizes(z, y)
    depth, count = unknowns // pairs, len(accs)
    return call(
        functools.partial(spread_kernel, rows, count), shape, count, count, 1,
        grid=(pairs,),
        in_specs=[z_spec(rows, depth, slot) for slot in range(1, 1 + count)]
        + [y_spec(depth, columns, pairs)]
        + [whole(rows, columns)] * count,
        out_specs=[whole(rows, columns)] * count,
        out_shape=[jax.ShapeDtypeStruct((rows, columns), jnp.float32)] * count,
    )(*([z] * count), y, *accs)


def step_kernel(
    pairs, flag_ref, z_ref, y_ref, base_ref, next_ref, loads_ref, drive_ref, send_ref,
    z_buf, y_buf, base_buf, next_buf, loads_buf, drive_buf, send_buf, z_sems, y_sems, sems,
):
    depth = z_buf.shape[1] // pairs
    copies = []
    for at, pair in enumerate(ring_of(pairs)):
        across, down = pl.ds(pair * depth, depth), pl.ds(at * depth, depth)
        copies.append((
            pltpu.make_async_copy(z_ref.at[0, :, across], z_buf.at[:, across], z_sems.at[at]),
            pltpu.make_async_copy(y_ref.at[down, :], y_buf.at[down, :], y_sems.at[at]),
        ))
    for z_copy, y_copy in copies:
        z_copy.start()
        y_copy.start()
    small = [
        pltpu.make_async_copy(base_ref, base_buf, sems.at[0]),
        pltpu.make_async_copy(next_ref, next_buf, sems.at[1]),
        pltpu.make_async_copy(loads_ref, loads_buf, sems.at[2]),
    ]
    for copy in small:
        copy.start()
    for at, pair in enumerate(ring_of(pairs)):
        for copy in copies[at]:
            copy.wait()
        term = dot(z_buf[:, pair * depth : (pair + 1) * depth], y_buf[at * depth : (at + 1) * depth])
        if at == 0:
            drive_buf[...] = term
        else:
            drive_buf[...] += term
    for copy in small:
        copy.wait()
    drive_buf[...] = base_buf[...] - drive_buf[...]
    drive_copy = pltpu.make_async_copy(drive_buf, drive_ref, sems.at[3])
    drive_copy.start()
    first = flag_ref[0] != 0
    lanes = loads_buf.shape[2]
    for start in range(0, drive_buf.shape[1], lanes):
        part = pl.ds(start, lanes)
        density = load_update(drive_buf[:, part], loads_buf[0], loads_buf[1])
        send_buf[:, part] = jnp.where(first, density, next_buf[:, part])
    send_copy = pltpu.make_async_copy(send_buf, send_ref, sems.at[4])
    send_copy.start()
    send_copy.wait()
    drive_copy.wait()


def step(pairs, flag, z, y, base, following, loads):
    rows, columns, unknowns = shape = sizes(z, y)
    hbm = pl.BlockSpec(memory_space=pl.ANY)
    return call(
        functools.partial(step_kernel, pairs), shape, 1, 1, 1,
        in_specs=[pl.BlockSpec(memory_space=pltpu.SMEM)] + [hbm] * 5,
        out_specs=[hbm, hbm],
        out_shape=[
            jax.ShapeDtypeStruct((rows, columns), jnp.float32),
            jax.ShapeDtypeStruct((rows, columns), jnp.bfloat16),
        ],
        scratch_shapes=[
            pltpu.VMEM((rows, unknowns), jnp.bfloat16),
            pltpu.VMEM((unknowns, columns), jnp.bfloat16),
            pltpu.VMEM((rows, columns), jnp.float32),
            pltpu.VMEM((rows, columns), jnp.bfloat16),
            pltpu.VMEM(loads.shape, jnp.float32),
            pltpu.VMEM((rows, columns), jnp.float32),
            pltpu.VMEM((rows, columns), jnp.bfloat16),
            pltpu.SemaphoreType.DMA((pairs,)),
            pltpu.SemaphoreType.DMA((pairs,)),
            pltpu.SemaphoreType.DMA((5,)),
        ],
    )(flag, z, y, base, following, loads)


def gather_rows(pairs, block, axis):
    order = [2 * pair + core for pair in ring_of(pairs) for core in (0, 1)]
    return lax.all_gather(block, "row", axis=axis, tiled=True, axis_index_groups=[order])


def two_group_body(pairs, lag_matrices, history, excitation, admittance, saturation):
    z, steps = lag_matrices, excitation.shape[0]
    slots = z.shape[0]
    is_first = lax.axis_index("lag") == 0
    flag = is_first.astype(jnp.int32)[None]
    admit_col, satur_col = admittance[:, None], saturation[:, None]
    lanes = math.gcd(128, excitation.shape[-1])
    loads = jnp.broadcast_to(jnp.stack([admit_col, satur_col]), (2, admit_col.shape[0], lanes))
    down, up = [(1, 0)], [(0, 1)]

    incoming = lax.ppermute(history[slots - (steps - 1) :], "lag", up)
    archive = gather_rows(pairs, history, 1)
    archive, incoming = lax.optimization_barrier((archive, incoming))
    ahead = gather_rows(pairs, incoming[steps - 2], 0)

    first_part = slots_product(pairs, z, archive, 0, slots)
    first_other = lax.ppermute(first_part, "lag", down)
    archive, first_part = lax.optimization_barrier((archive, first_part))
    part = slots_product(pairs, z, archive, 1, slots - 2)
    loads, part, first_part = lax.optimization_barrier((loads, part, first_part))
    density = load_update(excitation[0] - (first_part + first_other), admit_col, satur_col)
    send = jnp.where(is_first, density, incoming[steps - 3])
    results = [send]
    fresh = gather_rows(pairs, send, 0)

    ahead, send = lax.optimization_barrier((ahead, send))
    own = next_product(pairs, z, ahead, archive, slots - 2, part)
    other = lax.ppermute(own, "lag", down)
    archive, own = lax.optimization_barrier((archive, own))
    (theirs,) = later_products(pairs, z, ahead, archive, 0, 1)
    accs = []

    for index in range(1, steps):
        base = jnp.where(is_first, excitation[index] + other + own, theirs)
        coming = incoming[max(steps - 3 - index, 0)]
        drive, send = step(pairs, flag, z, fresh, base, coming, loads)
        results.append(send)
        if index + 1 < steps:
            rows_before = fresh
            fresh = gather_rows(pairs, send, 0)
            other = lax.ppermute(drive, "lag", down)
            rows_before, ahead, archive, send = lax.optimization_barrier(
                (rows_before, ahead, archive, send)
            )
            if index == 1:
                sums = [theirs] + list(later_products(pairs, z, ahead, archive, 1, steps - 2))
                accs = [
                    jnp.where(is_first, mine, sums[min(i + 1, steps - 3)])
                    for i, mine in enumerate(sums)
                ]
            accs = spread(pairs, z, rows_before, accs)
            own = theirs = accs[0]
            accs = accs[1:]

    early = jnp.stack(results[:-1])
    early = jnp.where(is_first, early, lax.ppermute(early, "lag", up))
    last = jnp.where(is_first, results[-1], lax.ppermute(results[-1], "lag", up))
    whole_run = jnp.concatenate([early, early[:1]], axis=0)
    return lax.dynamic_update_slice(whole_run, last[None], (steps - 1, 0, 0))


def general_body(lag_matrices, history, excitation, admittance, saturation):
    slot_count = lag_matrices.shape[0]
    step_count = excitation.shape[0]
    lag_index = lax.axis_index("lag")
    admit_col = admittance[:, None]
    satur_col = saturation[:, None]
    archive = lax.all_gather(history, "lag", axis=0, tiled=True)
    archive = lax.all_gather(archive, "row", axis=1, tiled=True)
    results = []
    for step_index in range(step_count):
        own_slots = lax.dynamic_slice_in_dim(archive, lag_index * slot_count, slot_count, 0)
        partial_sum = jnp.einsum(
            "lrm,lmc->rc", lag_matrices, own_slots, preferred_element_type=jnp.float32
        )
        summed = lax.psum(partial_sum, "lag")
        density = load_update(excitation[step_index] - summed, admit_col, satur_col)
        results.append(density)
        if step_index + 1 < step_count:
            full_density = lax.all_gather(density, "row", axis=0, tiled=True)
            archive = jnp.concatenate([full_density[None], archive[:-1]], axis=0)
    return jnp.stack(results)


def solution(mesh):
    groups, members = mesh.shape["lag"], mesh.shape["row"]
    placed = (
        P("lag", "row", None),
        P("lag", "row", None),
        P(None, "row", None),
        P("row"),
        P("row"),
    )

    def body(lag_matrices, history, excitation, admittance, saturation):
        slots, steps = lag_matrices.shape[0], excitation.shape[0]
        chosen = general_body
        depth = lag_matrices.shape[2] // members
        if groups == 2 and members % 4 == 0 and depth % 128 == 0 and 2 < steps <= slots:
            chosen = functools.partial(two_group_body, members // 2)
        return chosen(lag_matrices, history, excitation, admittance, saturation)

    return jax.shard_map(
        body, mesh=mesh, in_specs=placed, out_specs=P(None, "row", None), check_vma=False
    )
```

time: 294 us -> 283 us (0.963)
  waiting for transfers between devices: 129 us -> 116 us
  Pallas kernels: 116 us -> 121 us
    all_gather x5, waiting for transfers between devices: 104 us -> 92.8 us  [gather_rows(): lax.all_gather(block, 'row', axis=axis, tiled=True, axis_index_groups=[or...]
    pallas_call x5 -> x6, Pallas kernels: 56.6 us -> 64.8 us  [the longest x2 29.5 us: later_products(): call(functools.partial(later_kernel, rows, low, high, top), shape, produc...]
    sub x3 -> x0, other arithmetic: 5.8 us -> none  [two_group_body(): base = jnp.where(is_first, excitation[index] + other, 0.0) - accs[0]]
    select_n x0 -> x4, other arithmetic: none -> 5.73 us  [the longest x3 4.87 us: two_group_body(): base = jnp.where(is_first, excitation[index] + other + own, theirs)]
    pallas_call x2, Pallas kernels: 37.2 us -> 33.7 us  [slots_product(): call(functools.partial(slots_kernel, count), shape, count, count, count,...]
  transfers between devices with their start and end apart: 12 -> 12, of which waited for: 6 -> 7; matrix products, arithmetic and copies ran while one was open for 4% -> 4% of each run, Pallas kernels for 34% -> 38%
where the time goes in v3:
time: 283 us
  Pallas kernels  121 us (43%)
  waiting for transfers between devices  116 us (41%)
  starting transfers between devices  18.8 us (7%)
  between operations  13.4 us (5%)
  other arithmetic  10.5 us (4%)
  local copies, waits for them, and re-layouts  3.11 us (1%)
    all_gather x5, waiting for transfers between devices, gather_rows(): lax.all_gather(block, 'row', axis=axis, tiled=True, axis_index_groups=[or...  92.8 us
    pallas_call x2, Pallas kernels, slots_product(): call(functools.partial(slots_kernel, count), shape, count, count, count,...  33.7 us
    pallas_call x2, Pallas kernels, later_products(): call(functools.partial(later_kernel, rows, low, high, top), shape, produc...  29.5 us
    pallas_call x2, Pallas kernels, spread(): call(functools.partial(spread_kernel, rows, count), shape, count, count,...  22.6 us
    pallas_call x3, Pallas kernels, step(): call(functools.partial(step_kernel, pairs), shape, 1, 1, 1, in_specs=[pl....  22 us
    ppermute x1, waiting for transfers between devices, two_group_body(): incoming = lax.ppermute(history[slots - (steps - 1):], 'lag', up)  16.7 us
    pallas_call x1, Pallas kernels, next_product(): call(next_kernel, shape, 2, 2, 2, grid=(pairs,), in_specs=[z_spec(rows, d...  13.2 us
  transfers between devices with their start and end apart: 12, of which 7 were waited for; matrix products, arithmetic and copies ran while one was open for 4% of the time, Pallas kernels for 38%

profile of v3, /device:TPU:0, one launch (start us, length us, event | category | flops | bytes accessed | tf_op | source)
XLA Modules:
  0.0 282.7 jit_solution(2362605074736394695)
XLA Ops:
  8.5 4.9 %collective-permute-start = (bf16[3,512,256]{2,1,0:T(8,128)(2,1)S(1)}, bf16[3,512,256]{2,1,0:T(8,128)(2,1)S(1)}, u32[]{:S(2)}, u32[]{:S(2)}) collective-permute-start(bf16[3,512,256]{2,1,0:T(8,128)(2,1)S(1)} %slice.30), channel_id=1, source_target_pairs={{0,16},{1,17},{2,18},{3,19},{4,20},{5,21},{6,22},{7,23},{8,24},{9,... | collective-permute-start | bytes 2359304 | tf_op jit(solution)/shard_map/ppermute | solution.py:286
  13.4 16.7 %collective-permute-done = bf16[3,512,256]{2,1,0:T(8,128)(2,1)S(1)} collective-permute-done((bf16[3,512,256]{2,1,0:T(8,128)(2,1)S(1)}, bf16[3,512,256]{2,1,0:T(8,128)(2,1)S(1)}, u32[]{:S(2)}, u32[]{:S(2)}) %collective-permute-start) | collective-permute-done | bytes 786464 | tf_op jit(solution)/shard_map/ppermute | solution.py:286
  30.2 70.6 %all-gather.7.cloned.1.call-done.refs_4_.refs_2_.h_ref.refs_3_ = bf16[4,8192,256]{2,1,0:T(8,128)(2,1)} async-done(((bf16[4,512,256]{2,1,0:T(8,128)(2,1)}), bf16[4,8192,256]{2,1,0:T(8,128)(2,1)}) %all-gather.7.cloned.1.call-update) | async-done | bytes 16777232 | tf_op jit(solution)/shard_map/all_gather | solution.py:273
  101.7 20.4 %shard_map.55 = f32[512,256]{1,0:T(8,128)} custom-call(bf16[4,512,8192]{2,1,0:T(8,128)(2,1)} %z_ref.5, bf16[4,512,8192]{2,1,0:T(8,128)(2,1)} %z_ref.5, bf16[4,512,8192]{2,1,0:T(8,128)(2,1)} %z_ref.5, bf16[4,512,8192]{2,1,0:T(8,128)(2,1)} %z_ref.5, bf16[4,8192,256]{2,1,0:T(8,128)(2,1)} %all-gather.7.cloned.1.call-done.refs_4_.refs_2_.h_ref.refs_3_), custom_call_target="tpu_custom_call" | custom-call | flops 8589934592 | bytes 50331648 | tf_op jit(solution)/shard_map/pallas_call | solution.py:93
  123.4 13.3 %shard_map.56.part_ref = f32[512,256]{1,0:T(8,128)} custom-call(bf16[4,512,8192]{2,1,0:T(8,128)(2,1)} %z_ref.5, bf16[4,512,8192]{2,1,0:T(8,128)(2,1)} %z_ref.5, bf16[4,8192,256]{2,1,0:T(8,128)(2,1)} %all-gather.7.cloned.1.call-done.refs_4_.refs_2_.h_ref.refs_3_), custom_call_target="tpu_custom_call" | custom-call | flops 4294967296 | bytes 25165824 | tf_op jit(solution)/shard_map/pallas_call | solution.py:93
  139.3 13.2 %shard_map.57 = f32[512,256]{1,0:T(8,128)} custom-call(bf16[4,512,8192]{2,1,0:T(8,128)(2,1)} %z_ref.5, bf16[8192,256]{1,0:T(8,128)(2,1)} %bitcast.35, bf16[4,512,8192]{2,1,0:T(8,128)(2,1)} %z_ref.5, bf16[4,8192,256]{2,1,0:T(8,128)(2,1)} %all-gather.7.cloned.1.call-done.refs_4_.refs_2_.h_ref.refs_3_, f32[512,256]{1,0:T(8,128)} %shard_map.56.part_ref), custom_call_target="tpu_custom_call" | custom-call | flops 4294967296 | bytes 25165824 | tf_op jit(solution)/shard_map/pallas_call | solution.py:118
  152.5 1.4 collective-permute-start.2
  153.9 16.7 %shard_map.58 = f32[512,256]{1,0:T(8,128)} custom-call(bf16[4,512,8192]{2,1,0:T(8,128)(2,1)} %z_ref.5, bf16[4,512,8192]{2,1,0:T(8,128)(2,1)} %z_ref.5, bf16[4,512,8192]{2,1,0:T(8,128)(2,1)} %z_ref.5, bf16[8192,256]{1,0:T(8,128)(2,1)} %bitcast.36, bf16[4,8192,256]{2,1,0:T(8,128)(2,1)} %all-gather.7.cloned.1.call-done.refs_4_.refs_2_.h_ref.refs_3_), custom_call_target="tpu_custom_call" | custom-call | flops 6442450944 | bytes 37748736 | tf_op jit(solution)/shard_map/pallas_call | solution.py:157
  171.5 3.6 %all-gather.9.cloned.1.call-done.y_ref.refs_2_ = bf16[8192,256]{1,0:T(8,128)(2,1)} async-done(((bf16[512,256]{1,0:T(8,128)(2,1)}), bf16[8192,256]{1,0:T(8,128)(2,1)}) %all-gather.9.cloned.1.call-update) | async-done | bytes 4194320 | tf_op jit(solution)/shard_map/all_gather | solution.py:273
  175.1 7.4 %shard_map.59 = (f32[512,256]{1,0:T(8,128)}, bf16[512,256]{1,0:T(8,128)(2,1)}) custom-call(s32[1]{0:T(128)} %bitcast.6.flag_ref, bf16[4,512,8192]{2,1,0:T(8,128)(2,1)} %z_ref.5, bf16[8192,256]{1,0:T(8,128)(2,1)} %all-gather.9.cloned.1.call-done.y_ref.refs_2_, f32[512,256]{1,0:T(8,128)} %fusion.1.base_ref, bf16[512,256]{1,0:T(8,128)(2,1)} %get-tuple-element.47.next_ref, ...), custom_call_target="tpu_custom_call" | custom-call | flops 2147483648 | bytes 12582912 | tf_op jit(solution)/shard_map/pallas_call | solution.py:248
  182.6 1.4 collective-permute-start.3
  184.0 12.9 %shard_map.60.refs_4_ = f32[512,256]{1,0:T(8,128)} custom-call(bf16[4,512,8192]{2,1,0:T(8,128)(2,1)} %z_ref.5, bf16[4,512,8192]{2,1,0:T(8,128)(2,1)} %z_ref.5, bf16[8192,256]{1,0:T(8,128)(2,1)} %bitcast.37, bf16[4,8192,256]{2,1,0:T(8,128)(2,1)} %all-gather.7.cloned.1.call-done.refs_4_.refs_2_.h_ref.refs_3_), custom_call_target="tpu_custom_call" | custom-call | flops 4294967296 | bytes 25165824 | tf_op jit(solution)/shard_map/pallas_call | solution.py:157
  197.7 13.2 %shard_map.61 = (f32[512,256]{1,0:T(8,128)}, f32[512,256]{1,0:T(8,128)}) custom-call(bf16[4,512,8192]{2,1,0:T(8,128)(2,1)} %z_ref.5, bf16[4,512,8192]{2,1,0:T(8,128)(2,1)} %z_ref.5, bf16[8192,256]{1,0:T(8,128)(2,1)} %all-gather.9.cloned.1.call-done.y_ref.refs_2_, f32[512,256]{1,0:T(8,128)} %broadcast_select_fusion.1.refs_3_, f32[512,256]{1,0:T(8,128)} %shard_map.60.refs_4_), custom_call_target="tpu_custom_call" | custom-call | flops 4294967296 | bytes 20971520 | tf_op jit(solution)/shard_map/pallas_call | solution.py:187
  210.9 1.9 add_select_fusion.1.base_ref
  212.9 3.8 %all-gather.11.cloned.1.call-done.y_ref.refs_1_ = bf16[8192,256]{1,0:T(8,128)(2,1)} async-done(((bf16[512,256]{1,0:T(8,128)(2,1)}), bf16[8192,256]{1,0:T(8,128)(2,1)}) %all-gather.11.cloned.1.call-update) | async-done | bytes 4194320 | tf_op jit(solution)/shard_map/all_gather | solution.py:273
  216.7 7.3 %shard_map.62 = (f32[512,256]{1,0:T(8,128)}, bf16[512,256]{1,0:T(8,128)(2,1)}) custom-call(s32[1]{0:T(128)} %bitcast.6.flag_ref, bf16[4,512,8192]{2,1,0:T(8,128)(2,1)} %z_ref.5, bf16[8192,256]{1,0:T(8,128)(2,1)} %all-gather.11.cloned.1.call-done.y_ref.refs_1_, f32[512,256]{1,0:T(8,128)} %add_select_fusion.1.base_ref, ...), custom_call_target="tpu_custom_call" | custom-call | flops 2147483648 | bytes 12582912 | tf_op jit(solution)/shard_map/pallas_call | solution.py:248
  225.4 1.9 pad_maximum_fusion.1
  227.3 4.8 %collective-permute-start.4 = (bf16[3,512,256]{2,1,0:T(8,128)(2,1)}, bf16[3,512,256]{2,1,0:T(8,128)(2,1)S(1)}, u32[]{:S(2)}, u32[]{:S(2)}) collective-permute-start(bf16[3,512,256]{2,1,0:T(8,128)(2,1)} %pad_maximum_fusion.1), channel_id=1, source_target_pairs={{0,16},{1,17},{2,18},{3,19},{4,20},{5,21},{6,22},{7,23},{8,24},{9,... | collective-permute-start | bytes 2359304 | tf_op jit(solution)/shard_map/ppermute | solution.py:331
  232.1 9.4 %shard_map.63 = f32[512,256]{1,0:T(8,128)} custom-call(bf16[4,512,8192]{2,1,0:T(8,128)(2,1)} %z_ref.5, bf16[8192,256]{1,0:T(8,128)(2,1)} %all-gather.11.cloned.1.call-done.y_ref.refs_1_, f32[512,256]{1,0:T(8,128)} %get-tuple-element.45.refs_2_), custom_call_target="tpu_custom_call" | custom-call | flops 2147483648 | bytes 12582912 | tf_op jit(solution)/shard_map/pallas_call | solution.py:187
  241.5 1.9 add_select_fusion.base_ref
  243.4 14.8 %all-gather.13.cloned.1.call-done.y_ref = bf16[8192,256]{1,0:T(8,128)(2,1)} async-done(((bf16[512,256]{1,0:T(8,128)(2,1)}), bf16[8192,256]{1,0:T(8,128)(2,1)}) %all-gather.13.cloned.1.call-update) | async-done | bytes 4194320 | tf_op jit(solution)/shard_map/all_gather | solution.py:273
  258.2 7.3 %shard_map.64 = (f32[512,256]{1,0:T(8,128)}, bf16[512,256]{1,0:T(8,128)(2,1)}) custom-call(s32[1]{0:T(128)} %bitcast.6.flag_ref, bf16[4,512,8192]{2,1,0:T(8,128)(2,1)} %z_ref.5, bf16[8192,256]{1,0:T(8,128)(2,1)} %all-gather.13.cloned.1.call-done.y_ref, f32[512,256]{1,0:T(8,128)} %add_select_fusion.base_ref, bf16[512,256]{1,0:T(8,128)(2,1)} %get-tuple-element.47.next_ref, ...), custom_call_target="tpu_custom_call" | custom-call | flops 2147483648 | bytes 12582912 | tf_op jit(solution)/shard_map/pallas_call | solution.py:248
  265.6 3.5 %collective-permute-start.6 = (bf16[512,256]{1,0:T(8,128)(2,1)}, bf16[512,256]{1,0:T(8,128)(2,1)S(1)}, u32[]{:S(2)}, u32[]{:S(2)}) collective-permute-start(bf16[512,256]{1,0:T(8,128)(2,1)} %get-tuple-element.46), channel_id=1, source_target_pairs={{0,16},{1,17},{2,18},{3,19},{4,20},{5,21},{6,22},{7,23},{8,24},{9,... | collective-permute-start | bytes 786440 | tf_op jit(solution)/shard_map/ppermute | solution.py:332
  270.4 5.0 %collective-permute-done.6 = bf16[512,256]{1,0:T(8,128)(2,1)S(1)} collective-permute-done((bf16[512,256]{1,0:T(8,128)(2,1)}, bf16[512,256]{1,0:T(8,128)(2,1)S(1)}, u32[]{:S(2)}, u32[]{:S(2)}) %collective-permute-start.6) | collective-permute-done | bytes 262176 | tf_op jit(solution)/shard_map/ppermute | solution.py:332
  (49 shorter events, 11.9 us)
Async XLA Ops:
  6.5 94.2 %all-gather.7.cloned.1.call-start = ((), (), s32[]{:S(2)}) async-start(), calls=%async_computation | async-start | bytes 17825792 | tf_op jit(solution)/shard_map/all_gather | solution.py:273
  7.3 132.0 %all-gather.15.cloned.1.call-start = ((), (), s32[]{:S(2)}) async-start(), calls=%async_computation.4 | async-start | bytes 4456448 | tf_op jit(solution)/shard_map/all_gather | solution.py:273
  8.5 21.7 %collective-permute-start = (bf16[3,512,256]{2,1,0:T(8,128)(2,1)S(1)}, bf16[3,512,256]{2,1,0:T(8,128)(2,1)S(1)}, u32[]{:S(2)}, u32[]{:S(2)}) collective-permute-start(bf16[3,512,256]{2,1,0:T(8,128)(2,1)S(1)} %slice.30), channel_id=1, source_target_pairs={{0,16},{1,17},{2,18},{3,19},{4,20},{5,21},{6,22},{7,23},{8,24},{9,... | collective-permute-start | bytes 2359304 | tf_op jit(solution)/shard_map/ppermute | solution.py:286
  101.6 21.7 %copy-start.8 = (f32[512]{0:T(512)S(1)}, f32[512]{0:T(512)}, u32[]{:S(2)}) copy-start(f32[512]{0:T(512)} %param.9) | copy-start | bytes 6148
  101.6 21.7 %copy-start.9 = (f32[512]{0:T(512)S(1)}, f32[512]{0:T(512)}, u32[]{:S(2)}) copy-start(f32[512]{0:T(512)} %param.8) | copy-start | bytes 6148
  101.6 73.5 %all-gather.9.cloned.1.call-start = ((), (), s32[]{:S(2)}) async-start(), calls=%async_computation.1 | async-start | bytes 4456448 | tf_op jit(solution)/shard_map/all_gather | solution.py:273
  122.0 16.2 %collective-permute-start.1 = (f32[512,256]{1,0:T(8,128)}, f32[512,256]{1,0:T(8,128)S(1)}, u32[]{:S(2)}, u32[]{:S(2)}) collective-permute-start(f32[512,256]{1,0:T(8,128)} %shard_map.55), channel_id=1, source_target_pairs={{16,0},{17,1},{18,2},{19,3},{20,4},{21,5},{22,6},{23,7},{24,8},{25... | collective-permute-start | bytes 1572872 | tf_op jit(solution)/shard_map/ppermute | solution.py:292
  123.3 14.9 %copy-start.4 = (f32[512,256]{1,0:T(8,128)S(1)}, f32[512,256]{1,0:T(8,128)}, u32[]{:S(2)}) copy-start(f32[512,256]{1,0:T(8,128)} %shard_map.55) | copy-start | bytes 1572868
  123.4 14.9 %copy-start.6 = (f32[4,512,256]{2,1,0:T(8,128)S(1)}, f32[4,512,256]{2,1,0:T(8,128)}, u32[]{:S(2)}) copy-start(f32[4,512,256]{2,1,0:T(8,128)} %param.7) | copy-start | bytes 6291460
  139.2 77.5 %all-gather.11.cloned.1.call-start = ((), (), s32[]{:S(2)}) async-start(), calls=%async_computation.2 | async-start | bytes 4456448 | tf_op jit(solution)/shard_map/all_gather | solution.py:273
  152.5 18.1 %copy-start.5 = (f32[512,256]{1,0:T(8,128)S(1)}, f32[512,256]{1,0:T(8,128)}, u32[]{:S(2)}) copy-start(f32[512,256]{1,0:T(8,128)} %shard_map.57) | copy-start | bytes 1572868
  152.5 18.1 %collective-permute-start.2 = (f32[512,256]{1,0:T(8,128)}, f32[512,256]{1,0:T(8,128)S(1)}, u32[]{:S(2)}, u32[]{:S(2)}) collective-permute-start(f32[512,256]{1,0:T(8,128)} %shard_map.57), channel_id=1, source_target_pairs={{16,0},{17,1},{18,2},{19,3},{20,4},{21,5},{22,6},{23,7},{24,8},{25... | collective-permute-start | bytes 1572872 | tf_op jit(solution)/shard_map/ppermute | solution.py:303
  182.5 75.7 %all-gather.13.cloned.1.call-start = ((), (), s32[]{:S(2)}) async-start(), calls=%async_computation.3 | async-start | bytes 4456448 | tf_op jit(solution)/shard_map/all_gather | solution.py:273
  182.5 14.3 %copy-start = (f32[512,256]{1,0:T(8,128)S(1)}, f32[512,256]{1,0:T(8,128)}, u32[]{:S(2)}) copy-start(f32[512,256]{1,0:T(8,128)} %shard_map.58) | copy-start | bytes 1572868
  182.6 28.4 %collective-permute-start.3 = (f32[512,256]{1,0:T(8,128)}, f32[512,256]{1,0:T(8,128)S(1)}, u32[]{:S(2)}, u32[]{:S(2)}) collective-permute-start(f32[512,256]{1,0:T(8,128)} %get-tuple-element.37), channel_id=1, source_target_pairs={{16,0},{17,1},{18,2},{19,3},{20,4},{21,5},{22,6},{23,7},{24,8},{25... | collective-permute-start | bytes 1572872 | tf_op jit(solution)/shard_map/ppermute | solution.py:316
  212.9 12.5 %copy-start.1 = (bf16[512,256]{1,0:T(8,128)(2,1)S(1)}, bf16[512,256]{1,0:T(8,128)(2,1)}, u32[]{:S(2)}) copy-start(bf16[512,256]{1,0:T(8,128)(2,1)} %fusion.2) | copy-start | bytes 786436
  212.9 12.5 %copy-start.2 = (bf16[512,256]{1,0:T(8,128)(2,1)S(1)}, bf16[512,256]{1,0:T(8,128)(2,1)}, u32[]{:S(2)}) copy-start(bf16[512,256]{1,0:T(8,128)(2,1)} %get-tuple-element.36) | copy-start | bytes 786436
  224.1 17.5 %collective-permute-start.5 = (f32[512,256]{1,0:T(8,128)}, f32[512,256]{1,0:T(8,128)S(1)}, u32[]{:S(2)}, u32[]{:S(2)}) collective-permute-start(f32[512,256]{1,0:T(8,128)} %get-tuple-element.43), channel_id=1, source_target_pairs={{16,0},{17,1},{18,2},{19,3},{20,4},{21,5},{22,6},{23,7},{24,8},{25... | collective-permute-start | bytes 1572872 | tf_op jit(solution)/shard_map/ppermute | solution.py:316
  227.3 41.8 %collective-permute-start.4 = (bf16[3,512,256]{2,1,0:T(8,128)(2,1)}, bf16[3,512,256]{2,1,0:T(8,128)(2,1)S(1)}, u32[]{:S(2)}, u32[]{:S(2)}) collective-permute-start(bf16[3,512,256]{2,1,0:T(8,128)(2,1)} %pad_maximum_fusion.1), channel_id=1, source_target_pairs={{0,16},{1,17},{2,18},{3,19},{4,20},{5,21},{6,22},{7,23},{8,24},{9,... | collective-permute-start | bytes 2359304 | tf_op jit(solution)/shard_map/ppermute | solution.py:331
  243.4 25.7 %copy-start.3 = (bf16[512,256]{1,0:T(8,128)(2,1)S(1)}, bf16[512,256]{1,0:T(8,128)(2,1)}, u32[]{:S(2)}) copy-start(bf16[512,256]{1,0:T(8,128)(2,1)} %get-tuple-element.42) | copy-start | bytes 786436
  265.6 9.8 %copy-start.7 = (bf16[512,256]{1,0:T(8,128)(2,1)S(1)}, bf16[512,256]{1,0:T(8,128)(2,1)}, u32[]{:S(2)}) copy-start(bf16[512,256]{1,0:T(8,128)(2,1)} %get-tuple-element.46) | copy-start | bytes 786436
  265.6 9.8 %collective-permute-start.6 = (bf16[512,256]{1,0:T(8,128)(2,1)}, bf16[512,256]{1,0:T(8,128)(2,1)S(1)}, u32[]{:S(2)}, u32[]{:S(2)}) collective-permute-start(bf16[512,256]{1,0:T(8,128)(2,1)} %get-tuple-element.46), channel_id=1, source_target_pairs={{0,16},{1,17},{2,18},{3,19},{4,20},{5,21},{6,22},{7,23},{8,24},{9,... | collective-permute-start | bytes 786440 | tf_op jit(solution)/shard_map/ppermute | solution.py:332
Sparse Core Ops, SparseCore 0:
  8.9 91.7 all-gather.6
  102.3 34.9 all-gather.14
  139.3 35.7 all-gather.8
  182.6 34.0 all-gather.10
  224.2 34.0 all-gather.12

commit v4 on v3

--- a/solution.py
+++ b/solution.py
@@ -285,14 +285,14 @@
 
     incoming = lax.ppermute(history[slots - (steps - 1) :], "lag", up)
     archive = gather_rows(pairs, history, 1)
-    archive, incoming = lax.optimization_barrier((archive, incoming))
+    archive, *incoming = lax.optimization_barrier((archive, *incoming))
     ahead = gather_rows(pairs, incoming[steps - 2], 0)
 
     first_part = slots_product(pairs, z, archive, 0, slots)
     first_other = lax.ppermute(first_part, "lag", down)
     archive, first_part = lax.optimization_barrier((archive, first_part))
     part = slots_product(pairs, z, archive, 1, slots - 2)
-    loads, part, first_part = lax.optimization_barrier((loads, part, first_part))
+    part, first_part = lax.optimization_barrier((part, first_part))
     density = load_update(excitation[0] - (first_part + first_other), admit_col, satur_col)
     send = jnp.where(is_first, density, incoming[steps - 3])
     results = [send]
@@ -303,6 +303,7 @@
     other = lax.ppermute(own, "lag", down)
     archive, own = lax.optimization_barrier((archive, own))
     (theirs,) = later_products(pairs, z, ahead, archive, 0, 1)
+    theirs, loads = lax.optimization_barrier((theirs, loads))
     accs = []
 
     for index in range(1, steps):

time: 283 us -> 283 us (level)
  transfers between devices with their start and end apart: 12 -> 12, of which waited for: 7 -> 7; matrix products, arithmetic and copies ran while one was open for 4% -> 5% of each run, Pallas kernels for 38% -> 38%
where the time goes in v4:
time: 283 us; the launch traced here: 282 us
  Pallas kernels  121 us (43%)
  waiting for transfers between devices  116 us (41%)
  starting transfers between devices  18.8 us (7%)
  between operations  13.4 us (5%)
  other arithmetic  10.5 us (4%)
  local copies, waits for them, and re-layouts  3.16 us (1%)
    all_gather x5, waiting for transfers between devices, gather_rows(): lax.all_gather(block, 'row', axis=axis, tiled=True, axis_index_groups=[or...  91.6 us
    pallas_call x2, Pallas kernels, slots_product(): call(functools.partial(slots_kernel, count), shape, count, count, count,...  33.7 us
    pallas_call x2, Pallas kernels, later_products(): call(functools.partial(later_kernel, rows, low, high, top), shape, produc...  29.4 us
    pallas_call x2, Pallas kernels, spread(): call(functools.partial(spread_kernel, rows, count), shape, count, count,...  22.7 us
    pallas_call x3, Pallas kernels, step(): call(functools.partial(step_kernel, pairs), shape, 1, 1, 1, in_specs=[pl....  22 us
    ppermute x1, waiting for transfers between devices, two_group_body(): incoming = lax.ppermute(history[slots - (steps - 1):], 'lag', up)  16.7 us
    pallas_call x1, Pallas kernels, next_product(): call(next_kernel, shape, 2, 2, 2, grid=(pairs,), in_specs=[z_spec(rows, d...  13.2 us
  transfers between devices with their start and end apart: 12, of which 7 were waited for; matrix products, arithmetic and copies ran while one was open for 5% of the time, Pallas kernels for 38%

profile of v4, /device:TPU:0, one launch (start us, length us, event | category | flops | bytes accessed | tf_op | source)
XLA Modules:
  0.0 282.5 jit_solution(10075292087341312882)
XLA Ops:
  8.5 4.9 %collective-permute-start = (bf16[3,512,256]{2,1,0:T(8,128)(2,1)S(1)}, bf16[3,512,256]{2,1,0:T(8,128)(2,1)S(1)}, u32[]{:S(2)}, u32[]{:S(2)}) collective-permute-start(bf16[3,512,256]{2,1,0:T(8,128)(2,1)S(1)} %slice.19), channel_id=1, source_target_pairs={{0,16},{1,17},{2,18},{3,19},{4,20},{5,21},{6,22},{7,23},{8,24},{9,... | collective-permute-start | bytes 2359304 | tf_op jit(solution)/shard_map/ppermute | solution.py:286
  13.4 16.7 %collective-permute-done = bf16[3,512,256]{2,1,0:T(8,128)(2,1)S(1)} collective-permute-done((bf16[3,512,256]{2,1,0:T(8,128)(2,1)S(1)}, bf16[3,512,256]{2,1,0:T(8,128)(2,1)S(1)}, u32[]{:S(2)}, u32[]{:S(2)}) %collective-permute-start) | collective-permute-done | bytes 786464 | tf_op jit(solution)/shard_map/ppermute | solution.py:286
  31.0 69.7 %all-gather.6.cloned.1.call-done.refs_4_.refs_2_.h_ref.refs_3_ = bf16[4,8192,256]{2,1,0:T(8,128)(2,1)} async-done(((bf16[4,512,256]{2,1,0:T(8,128)(2,1)}), bf16[4,8192,256]{2,1,0:T(8,128)(2,1)}) %all-gather.6.cloned.1.call-update) | async-done | bytes 16777232 | tf_op jit(solution)/shard_map/all_gather | solution.py:273
  100.8 20.4 %shard_map.55 = f32[512,256]{1,0:T(8,128)} custom-call(bf16[4,512,8192]{2,1,0:T(8,128)(2,1)} %z_ref.5, bf16[4,512,8192]{2,1,0:T(8,128)(2,1)} %z_ref.5, bf16[4,512,8192]{2,1,0:T(8,128)(2,1)} %z_ref.5, bf16[4,512,8192]{2,1,0:T(8,128)(2,1)} %z_ref.5, bf16[4,8192,256]{2,1,0:T(8,128)(2,1)} %all-gather.6.cloned.1.call-done.refs_4_.refs_2_.h_ref.refs_3_), custom_call_target="tpu_custom_call" | custom-call | flops 8589934592 | bytes 50331648 | tf_op jit(solution)/shard_map/pallas_call | solution.py:93
  122.5 13.3 %shard_map.56.part_ref = f32[512,256]{1,0:T(8,128)} custom-call(bf16[4,512,8192]{2,1,0:T(8,128)(2,1)} %z_ref.5, bf16[4,512,8192]{2,1,0:T(8,128)(2,1)} %z_ref.5, bf16[4,8192,256]{2,1,0:T(8,128)(2,1)} %all-gather.6.cloned.1.call-done.refs_4_.refs_2_.h_ref.refs_3_), custom_call_target="tpu_custom_call" | custom-call | flops 4294967296 | bytes 25165824 | tf_op jit(solution)/shard_map/pallas_call | solution.py:93
  135.8 1.5 collective-permute-done.1
  138.4 13.2 %shard_map.57 = f32[512,256]{1,0:T(8,128)} custom-call(bf16[4,512,8192]{2,1,0:T(8,128)(2,1)} %z_ref.5, bf16[8192,256]{1,0:T(8,128)(2,1)} %all-gather.10.cloned.1.call-done.y_ref.refs_3_.refs_2_, bf16[4,512,8192]{2,1,0:T(8,128)(2,1)} %z_ref.5, bf16[4,8192,256]{2,1,0:T(8,128)(2,1)} %all-gather.6.cloned.1.call-done.refs_4_.refs_2_.h_ref.refs_3_, ...), custom_call_target="tpu_custom_call" | custom-call | flops 4294967296 | bytes 25165824 | tf_op jit(solution)/shard_map/pallas_call | solution.py:118
  153.1 16.6 %shard_map.58 = f32[512,256]{1,0:T(8,128)} custom-call(bf16[4,512,8192]{2,1,0:T(8,128)(2,1)} %z_ref.5, bf16[4,512,8192]{2,1,0:T(8,128)(2,1)} %z_ref.5, bf16[4,512,8192]{2,1,0:T(8,128)(2,1)} %z_ref.5, bf16[8192,256]{1,0:T(8,128)(2,1)} %all-gather.10.cloned.1.call-done.y_ref.refs_3_.refs_2_, ...), custom_call_target="tpu_custom_call" | custom-call | flops 6442450944 | bytes 37748736 | tf_op jit(solution)/shard_map/pallas_call | solution.py:157
  171.7 1.5 all-gather.8.cloned.1.call-done.y_ref.refs_2_
  173.2 7.4 %shard_map.59 = (f32[512,256]{1,0:T(8,128)}, bf16[512,256]{1,0:T(8,128)(2,1)}) custom-call(s32[1]{0:T(128)} %bitcast.5.flag_ref, bf16[4,512,8192]{2,1,0:T(8,128)(2,1)} %z_ref.5, bf16[8192,256]{1,0:T(8,128)(2,1)} %all-gather.8.cloned.1.call-done.y_ref.refs_2_, f32[512,256]{1,0:T(8,128)} %fusion.1.base_ref, bf16[512,256]{1,0:T(8,128)(2,1)} %get-tuple-element.40.next_ref, ...), custom_call_target="tpu_custom_call" | custom-call | flops 2147483648 | bytes 12582912 | tf_op jit(solution)/shard_map/pallas_call | solution.py:248
  180.7 1.4 collective-permute-start.3
  182.1 12.8 %shard_map.60.refs_4_ = f32[512,256]{1,0:T(8,128)} custom-call(bf16[4,512,8192]{2,1,0:T(8,128)(2,1)} %z_ref.5, bf16[4,512,8192]{2,1,0:T(8,128)(2,1)} %z_ref.5, bf16[8192,256]{1,0:T(8,128)(2,1)} %all-gather.10.cloned.1.call-done.y_ref.refs_3_.refs_2_, bf16[4,8192,256]{2,1,0:T(8,128)(2,1)} %all-gather.6.cloned.1.call-done.refs_4_.refs_2_.h_ref.refs_3_), custom_call_target="tpu_custom_call" | custom-call | flops 4294967296 | bytes 25165824 | tf_op jit(solution)/shard_map/pallas_call | solution.py:157
  195.7 13.3 %shard_map.61 = (f32[512,256]{1,0:T(8,128)}, f32[512,256]{1,0:T(8,128)}) custom-call(bf16[4,512,8192]{2,1,0:T(8,128)(2,1)} %z_ref.5, bf16[4,512,8192]{2,1,0:T(8,128)(2,1)} %z_ref.5, bf16[8192,256]{1,0:T(8,128)(2,1)} %all-gather.8.cloned.1.call-done.y_ref.refs_2_, f32[512,256]{1,0:T(8,128)} %broadcast_select_fusion.1.refs_3_, f32[512,256]{1,0:T(8,128)} %shard_map.60.refs_4_), custom_call_target="tpu_custom_call" | custom-call | flops 4294967296 | bytes 20971520 | tf_op jit(solution)/shard_map/pallas_call | solution.py:187
  209.0 1.9 add_select_fusion.1.base_ref
  211.0 5.5 %all-gather.12.cloned.1.call-done.y_ref.refs_1_ = bf16[8192,256]{1,0:T(8,128)(2,1)} async-done(((bf16[512,256]{1,0:T(8,128)(2,1)}), bf16[8192,256]{1,0:T(8,128)(2,1)}) %all-gather.12.cloned.1.call-update) | async-done | bytes 4194320 | tf_op jit(solution)/shard_map/all_gather | solution.py:273
  216.5 7.3 %shard_map.62 = (f32[512,256]{1,0:T(8,128)}, bf16[512,256]{1,0:T(8,128)(2,1)}) custom-call(s32[1]{0:T(128)} %bitcast.5.flag_ref, bf16[4,512,8192]{2,1,0:T(8,128)(2,1)} %z_ref.5, bf16[8192,256]{1,0:T(8,128)(2,1)} %all-gather.12.cloned.1.call-done.y_ref.refs_1_, f32[512,256]{1,0:T(8,128)} %add_select_fusion.1.base_ref, ...), custom_call_target="tpu_custom_call" | custom-call | flops 2147483648 | bytes 12582912 | tf_op jit(solution)/shard_map/pallas_call | solution.py:248
  225.2 1.9 pad_maximum_fusion.1
  227.1 4.8 %collective-permute-start.4 = (bf16[3,512,256]{2,1,0:T(8,128)(2,1)}, bf16[3,512,256]{2,1,0:T(8,128)(2,1)S(1)}, u32[]{:S(2)}, u32[]{:S(2)}) collective-permute-start(bf16[3,512,256]{2,1,0:T(8,128)(2,1)} %pad_maximum_fusion.1), channel_id=1, source_target_pairs={{0,16},{1,17},{2,18},{3,19},{4,20},{5,21},{6,22},{7,23},{8,24},{9,... | collective-permute-start | bytes 2359304 | tf_op jit(solution)/shard_map/ppermute | solution.py:332
  231.9 9.4 %shard_map.63 = f32[512,256]{1,0:T(8,128)} custom-call(bf16[4,512,8192]{2,1,0:T(8,128)(2,1)} %z_ref.5, bf16[8192,256]{1,0:T(8,128)(2,1)} %all-gather.12.cloned.1.call-done.y_ref.refs_1_, f32[512,256]{1,0:T(8,128)} %get-tuple-element.51.refs_2_), custom_call_target="tpu_custom_call" | custom-call | flops 2147483648 | bytes 12582912 | tf_op jit(solution)/shard_map/pallas_call | solution.py:187
  241.3 1.9 add_select_fusion.base_ref
  243.3 14.8 %all-gather.14.cloned.1.call-done.y_ref = bf16[8192,256]{1,0:T(8,128)(2,1)} async-done(((bf16[512,256]{1,0:T(8,128)(2,1)}), bf16[8192,256]{1,0:T(8,128)(2,1)}) %all-gather.14.cloned.1.call-update) | async-done | bytes 4194320 | tf_op jit(solution)/shard_map/all_gather | solution.py:273
  258.1 7.3 %shard_map.64 = (f32[512,256]{1,0:T(8,128)}, bf16[512,256]{1,0:T(8,128)(2,1)}) custom-call(s32[1]{0:T(128)} %bitcast.5.flag_ref, bf16[4,512,8192]{2,1,0:T(8,128)(2,1)} %z_ref.5, bf16[8192,256]{1,0:T(8,128)(2,1)} %all-gather.14.cloned.1.call-done.y_ref, f32[512,256]{1,0:T(8,128)} %add_select_fusion.base_ref, bf16[512,256]{1,0:T(8,128)(2,1)} %get-tuple-element.40.next_ref, ...), custom_call_target="tpu_custom_call" | custom-call | flops 2147483648 | bytes 12582912 | tf_op jit(solution)/shard_map/pallas_call | solution.py:248
  265.4 3.5 %collective-permute-start.6 = (bf16[512,256]{1,0:T(8,128)(2,1)}, bf16[512,256]{1,0:T(8,128)(2,1)S(1)}, u32[]{:S(2)}, u32[]{:S(2)}) collective-permute-start(bf16[512,256]{1,0:T(8,128)(2,1)} %get-tuple-element.52), channel_id=1, source_target_pairs={{0,16},{1,17},{2,18},{3,19},{4,20},{5,21},{6,22},{7,23},{8,24},{9,... | collective-permute-start | bytes 786440 | tf_op jit(solution)/shard_map/ppermute | solution.py:333
  270.2 5.0 %collective-permute-done.6 = bf16[512,256]{1,0:T(8,128)(2,1)S(1)} collective-permute-done((bf16[512,256]{1,0:T(8,128)(2,1)}, bf16[512,256]{1,0:T(8,128)(2,1)S(1)}, u32[]{:S(2)}, u32[]{:S(2)}) %collective-permute-start.6) | collective-permute-done | bytes 262176 | tf_op jit(solution)/shard_map/ppermute | solution.py:333
  (49 shorter events, 12.8 us)
Async XLA Ops:
  6.5 94.2 %all-gather.6.cloned.1.call-start = ((), (), s32[]{:S(2)}) async-start(), calls=%async_computation | async-start | bytes 17825792 | tf_op jit(solution)/shard_map/all_gather | solution.py:273
  7.3 131.1 %all-gather.10.cloned.1.call-start = ((), (), s32[]{:S(2)}) async-start(), calls=%async_computation.2 | async-start | bytes 4456448 | tf_op jit(solution)/shard_map/all_gather | solution.py:273
  8.5 21.7 %collective-permute-start = (bf16[3,512,256]{2,1,0:T(8,128)(2,1)S(1)}, bf16[3,512,256]{2,1,0:T(8,128)(2,1)S(1)}, u32[]{:S(2)}, u32[]{:S(2)}) collective-permute-start(bf16[3,512,256]{2,1,0:T(8,128)(2,1)S(1)} %slice.19), channel_id=1, source_target_pairs={{0,16},{1,17},{2,18},{3,19},{4,20},{5,21},{6,22},{7,23},{8,24},{9,... | collective-permute-start | bytes 2359304 | tf_op jit(solution)/shard_map/ppermute | solution.py:286
  100.7 72.5 %all-gather.8.cloned.1.call-start = ((), (), s32[]{:S(2)}) async-start(), calls=%async_computation.1 | async-start | bytes 4456448 | tf_op jit(solution)/shard_map/all_gather | solution.py:273
  121.2 16.2 %collective-permute-start.1 = (f32[512,256]{1,0:T(8,128)}, f32[512,256]{1,0:T(8,128)S(1)}, u32[]{:S(2)}, u32[]{:S(2)}) collective-permute-start(f32[512,256]{1,0:T(8,128)} %shard_map.55), channel_id=1, source_target_pairs={{16,0},{17,1},{18,2},{19,3},{20,4},{21,5},{22,6},{23,7},{24,8},{25... | collective-permute-start | bytes 1572872 | tf_op jit(solution)/shard_map/ppermute | solution.py:292
  122.5 14.9 %copy-start.4 = (f32[512,256]{1,0:T(8,128)S(1)}, f32[512,256]{1,0:T(8,128)}, u32[]{:S(2)}) copy-start(f32[512,256]{1,0:T(8,128)} %shard_map.55) | copy-start | bytes 1572868
  122.5 14.9 %copy-start.6 = (f32[4,512,256]{2,1,0:T(8,128)S(1)}, f32[4,512,256]{2,1,0:T(8,128)}, u32[]{:S(2)}) copy-start(f32[4,512,256]{2,1,0:T(8,128)} %param.7) | copy-start | bytes 6291460
  122.5 14.9 %copy-start.8 = (f32[512]{0:T(512)S(1)}, f32[512]{0:T(512)}, u32[]{:S(2)}) copy-start(f32[512]{0:T(512)} %param.9) | copy-start | bytes 6148
  122.5 14.8 %copy-start.9 = (f32[512]{0:T(512)S(1)}, f32[512]{0:T(512)}, u32[]{:S(2)}) copy-start(f32[512]{0:T(512)} %param.8) | copy-start | bytes 6148
  138.3 78.2 %all-gather.12.cloned.1.call-start = ((), (), s32[]{:S(2)}) async-start(), calls=%async_computation.3 | async-start | bytes 4456448 | tf_op jit(solution)/shard_map/all_gather | solution.py:273
  151.6 19.1 %copy-start.5 = (f32[512,256]{1,0:T(8,128)S(1)}, f32[512,256]{1,0:T(8,128)}, u32[]{:S(2)}) copy-start(f32[512,256]{1,0:T(8,128)} %shard_map.57) | copy-start | bytes 1572868
  151.7 19.0 %collective-permute-start.2 = (f32[512,256]{1,0:T(8,128)}, f32[512,256]{1,0:T(8,128)S(1)}, u32[]{:S(2)}, u32[]{:S(2)}) collective-permute-start(f32[512,256]{1,0:T(8,128)} %shard_map.57), channel_id=1, source_target_pairs={{16,0},{17,1},{18,2},{19,3},{20,4},{21,5},{22,6},{23,7},{24,8},{25... | collective-permute-start | bytes 1572872 | tf_op jit(solution)/shard_map/ppermute | solution.py:303
  180.6 77.5 %all-gather.14.cloned.1.call-start = ((), (), s32[]{:S(2)}) async-start(), calls=%async_computation.4 | async-start | bytes 4456448 | tf_op jit(solution)/shard_map/all_gather | solution.py:273
  180.6 14.2 %copy-start = (f32[512,256]{1,0:T(8,128)S(1)}, f32[512,256]{1,0:T(8,128)}, u32[]{:S(2)}) copy-start(f32[512,256]{1,0:T(8,128)} %shard_map.58) | copy-start | bytes 1572868
  180.7 28.4 %collective-permute-start.3 = (f32[512,256]{1,0:T(8,128)}, f32[512,256]{1,0:T(8,128)S(1)}, u32[]{:S(2)}, u32[]{:S(2)}) collective-permute-start(f32[512,256]{1,0:T(8,128)} %get-tuple-element.43), channel_id=1, source_target_pairs={{16,0},{17,1},{18,2},{19,3},{20,4},{21,5},{22,6},{23,7},{24,8},{25... | collective-permute-start | bytes 1572872 | tf_op jit(solution)/shard_map/ppermute | solution.py:317
  211.0 14.2 %copy-start.1 = (bf16[512,256]{1,0:T(8,128)(2,1)S(1)}, bf16[512,256]{1,0:T(8,128)(2,1)}, u32[]{:S(2)}) copy-start(bf16[512,256]{1,0:T(8,128)(2,1)} %fusion.2) | copy-start | bytes 786436
  211.0 14.2 %copy-start.2 = (bf16[512,256]{1,0:T(8,128)(2,1)S(1)}, bf16[512,256]{1,0:T(8,128)(2,1)}, u32[]{:S(2)}) copy-start(bf16[512,256]{1,0:T(8,128)(2,1)} %get-tuple-element.42) | copy-start | bytes 786436
  223.9 17.5 %collective-permute-start.5 = (f32[512,256]{1,0:T(8,128)}, f32[512,256]{1,0:T(8,128)S(1)}, u32[]{:S(2)}, u32[]{:S(2)}) collective-permute-start(f32[512,256]{1,0:T(8,128)} %get-tuple-element.49), channel_id=1, source_target_pairs={{16,0},{17,1},{18,2},{19,3},{20,4},{21,5},{22,6},{23,7},{24,8},{25... | collective-permute-start | bytes 1572872 | tf_op jit(solution)/shard_map/ppermute | solution.py:317
  227.1 41.8 %collective-permute-start.4 = (bf16[3,512,256]{2,1,0:T(8,128)(2,1)}, bf16[3,512,256]{2,1,0:T(8,128)(2,1)S(1)}, u32[]{:S(2)}, u32[]{:S(2)}) collective-permute-start(bf16[3,512,256]{2,1,0:T(8,128)(2,1)} %pad_maximum_fusion.1), channel_id=1, source_target_pairs={{0,16},{1,17},{2,18},{3,19},{4,20},{5,21},{6,22},{7,23},{8,24},{9,... | collective-permute-start | bytes 2359304 | tf_op jit(solution)/shard_map/ppermute | solution.py:332
  243.3 25.7 %copy-start.3 = (bf16[512,256]{1,0:T(8,128)(2,1)S(1)}, bf16[512,256]{1,0:T(8,128)(2,1)}, u32[]{:S(2)}) copy-start(bf16[512,256]{1,0:T(8,128)(2,1)} %get-tuple-element.48) | copy-start | bytes 786436
  265.4 9.8 %copy-start.7 = (bf16[512,256]{1,0:T(8,128)(2,1)S(1)}, bf16[512,256]{1,0:T(8,128)(2,1)}, u32[]{:S(2)}) copy-start(bf16[512,256]{1,0:T(8,128)(2,1)} %get-tuple-element.52) | copy-start | bytes 786436
  265.4 9.8 %collective-permute-start.6 = (bf16[512,256]{1,0:T(8,128)(2,1)}, bf16[512,256]{1,0:T(8,128)(2,1)S(1)}, u32[]{:S(2)}, u32[]{:S(2)}) collective-permute-start(bf16[512,256]{1,0:T(8,128)(2,1)} %get-tuple-element.52), channel_id=1, source_target_pairs={{0,16},{1,17},{2,18},{3,19},{4,20},{5,21},{6,22},{7,23},{8,24},{9,... | collective-permute-start | bytes 786440 | tf_op jit(solution)/shard_map/ppermute | solution.py:333
Sparse Core Ops, SparseCore 0:
  8.9 91.7 all-gather.5
  102.3 34.9 all-gather.9
  138.9 34.2 all-gather.7
  180.7 35.7 all-gather.11
  224.0 34.0 all-gather.13

commit v5 on v4

--- a/solution.py
+++ b/solution.py
@@ -196,7 +196,7 @@
 
 
 def step_kernel(
-    pairs, flag_ref, z_ref, y_ref, base_ref, next_ref, loads_ref, drive_ref, send_ref,
+    pairs, last, flag_ref, z_ref, y_ref, base_ref, next_ref, loads_ref, send_ref, drive_ref,
     z_buf, y_buf, base_buf, next_buf, loads_buf, drive_buf, send_buf, z_sems, y_sems, sems,
 ):
     depth = z_buf.shape[1] // pairs
@@ -228,8 +228,9 @@
     for copy in small:
         copy.wait()
     drive_buf[...] = base_buf[...] - drive_buf[...]
-    drive_copy = pltpu.make_async_copy(drive_buf, drive_ref, sems.at[3])
-    drive_copy.start()
+    if not last:
+        drive_copy = pltpu.make_async_copy(drive_buf, drive_ref, sems.at[3])
+        drive_copy.start()
     first = flag_ref[0] != 0
     lanes = loads_buf.shape[2]
     for start in range(0, drive_buf.shape[1], lanes):
@@ -239,20 +240,29 @@
     send_copy = pltpu.make_async_copy(send_buf, send_ref, sems.at[4])
     send_copy.start()
     send_copy.wait()
-    drive_copy.wait()
-
-
-def step(pairs, flag, z, y, base, following, loads):
+    if not last:
+        drive_copy.wait()
+
+
+def last_step_kernel(pairs, *refs):
+    step_kernel(pairs, True, *refs[:7], None, *refs[7:])
+
+
+def step(pairs, flag, z, y, base, following, loads, last):
     rows, columns, unknowns = shape = sizes(z, y)
     hbm = pl.BlockSpec(memory_space=pl.ANY)
-    return call(
-        functools.partial(step_kernel, pairs), shape, 1, 1, 1,
+    outs = [
+        jax.ShapeDtypeStruct((rows, columns), jnp.bfloat16),
+        jax.ShapeDtypeStruct((rows, columns), jnp.float32),
+    ]
+    kernel = functools.partial(step_kernel, pairs, False)
+    if last:
+        kernel, outs = functools.partial(last_step_kernel, pairs), outs[:1]
+    return call(
+        kernel, shape, 1, 1, 1,
         in_specs=[pl.BlockSpec(memory_space=pltpu.SMEM)] + [hbm] * 5,
-        out_specs=[hbm, hbm],
-        out_shape=[
-            jax.ShapeDtypeStruct((rows, columns), jnp.float32),
-            jax.ShapeDtypeStruct((rows, columns), jnp.bfloat16),
-        ],
+        out_specs=[hbm] * len(outs),
+        out_shape=outs,
         scratch_shapes=[
             pltpu.VMEM((rows, unknowns), jnp.bfloat16),
             pltpu.VMEM((unknowns, columns), jnp.bfloat16),
@@ -309,12 +319,12 @@
     for index in range(1, steps):
         base = jnp.where(is_first, excitation[index] + other + own, theirs)
         coming = incoming[max(steps - 3 - index, 0)]
-        drive, send = step(pairs, flag, z, fresh, base, coming, loads)
+        send, *drive = step(pairs, flag, z, fresh, base, coming, loads, index + 1 == steps)
         results.append(send)
         if index + 1 < steps:
             rows_before = fresh
             fresh = gather_rows(pairs, send, 0)
-            other = lax.ppermute(drive, "lag", down)
+            other = lax.ppermute(drive[0], "lag", down)
             rows_before, ahead, archive, send = lax.optimization_barrier(
                 (rows_before, ahead, archive, send)
             )
@@ -372,7 +382,7 @@
         slots, steps = lag_matrices.shape[0], excitation.shape[0]
         chosen = general_body
         depth = lag_matrices.shape[2] // members
-        if groups == 2 and members % 4 == 0 and depth % 128 == 0 and 2 < steps <= slots:
+        if groups == 2 and members % 4 == 0 and depth % 128 == 0 and 3 < steps <= slots:
             chosen = functools.partial(two_group_body, members // 2)
         return chosen(lag_matrices, history, excitation, admittance, saturation)
 

time: 283 us -> 283 us (level)
  no operation moved by 1% of the time
where the time goes in v5:
time: 283 us; the launch traced here: 282 us
  Pallas kernels  121 us (43%)
  waiting for transfers between devices  116 us (41%)
  starting transfers between devices  18.8 us (7%)
  between operations  13.4 us (5%)
  other arithmetic  10.5 us (4%)
  local copies, waits for them, and re-layouts  3.14 us (1%)
    all_gather x5, waiting for transfers between devices, gather_rows(): lax.all_gather(block, 'row', axis=axis, tiled=True, axis_index_groups=[or...  91.6 us
    pallas_call x2, Pallas kernels, slots_product(): call(functools.partial(slots_kernel, count), shape, count, count, count,...  33.7 us
    pallas_call x2, Pallas kernels, later_products(): call(functools.partial(later_kernel, rows, low, high, top), shape, produc...  29.3 us
    pallas_call x2, Pallas kernels, spread(): call(functools.partial(spread_kernel, rows, count), shape, count, count,...  22.7 us
    pallas_call x3, Pallas kernels, step(): call(kernel, shape, 1, 1, 1, in_specs=[pl.BlockSpec(memory_space=pltpu.SM...  21.9 us
    ppermute x1, waiting for transfers between devices, two_group_body(): incoming = lax.ppermute(history[slots - (steps - 1):], 'lag', up)  16.7 us
    pallas_call x1, Pallas kernels, next_product(): call(next_kernel, shape, 2, 2, 2, grid=(pairs,), in_specs=[z_spec(rows, d...  13.2 us
  transfers between devices with their start and end apart: 12, of which 7 were waited for; matrix products, arithmetic and copies ran while one was open for 5% of the time, Pallas kernels for 38%

profile of v5, /device:TPU:0, one launch (start us, length us, event | category | flops | bytes accessed | tf_op | source)
XLA Modules:
  0.0 282.4 jit_solution(2922531785574389987)
XLA Ops:
  8.5 4.9 %collective-permute-start = (bf16[3,512,256]{2,1,0:T(8,128)(2,1)S(1)}, bf16[3,512,256]{2,1,0:T(8,128)(2,1)S(1)}, u32[]{:S(2)}, u32[]{:S(2)}) collective-permute-start(bf16[3,512,256]{2,1,0:T(8,128)(2,1)S(1)} %slice.19), channel_id=1, source_target_pairs={{0,16},{1,17},{2,18},{3,19},{4,20},{5,21},{6,22},{7,23},{8,24},{9,... | collective-permute-start | bytes 2359304 | tf_op jit(solution)/shard_map/ppermute | solution.py:296
  13.4 16.7 %collective-permute-done = bf16[3,512,256]{2,1,0:T(8,128)(2,1)S(1)} collective-permute-done((bf16[3,512,256]{2,1,0:T(8,128)(2,1)S(1)}, bf16[3,512,256]{2,1,0:T(8,128)(2,1)S(1)}, u32[]{:S(2)}, u32[]{:S(2)}) %collective-permute-start) | collective-permute-done | bytes 786464 | tf_op jit(solution)/shard_map/ppermute | solution.py:296
  31.0 69.7 %all-gather.6.cloned.1.call-done.refs_4_.refs_2_.h_ref.refs_3_ = bf16[4,8192,256]{2,1,0:T(8,128)(2,1)} async-done(((bf16[4,512,256]{2,1,0:T(8,128)(2,1)}), bf16[4,8192,256]{2,1,0:T(8,128)(2,1)}) %all-gather.6.cloned.1.call-update) | async-done | bytes 16777232 | tf_op jit(solution)/shard_map/all_gather | solution.py:283
  100.8 20.4 %shard_map.55 = f32[512,256]{1,0:T(8,128)} custom-call(bf16[4,512,8192]{2,1,0:T(8,128)(2,1)} %refs_1_.11, bf16[4,512,8192]{2,1,0:T(8,128)(2,1)} %refs_1_.11, bf16[4,512,8192]{2,1,0:T(8,128)(2,1)} %refs_1_.11, bf16[4,512,8192]{2,1,0:T(8,128)(2,1)} %refs_1_.11, bf16[4,8192,256]{2,1,0:T(8,128)(2,1)} %all-gather.6.cloned.1.call-done.refs_4_.refs_2_.h_ref.refs_3_), custom_call_target="tpu_custom_call" | custom-call | flops 8589934592 | bytes 50331648 | tf_op jit(solution)/shard_map/pallas_call | solution.py:93
  122.5 13.3 %shard_map.56.part_ref = f32[512,256]{1,0:T(8,128)} custom-call(bf16[4,512,8192]{2,1,0:T(8,128)(2,1)} %refs_1_.11, bf16[4,512,8192]{2,1,0:T(8,128)(2,1)} %refs_1_.11, bf16[4,8192,256]{2,1,0:T(8,128)(2,1)} %all-gather.6.cloned.1.call-done.refs_4_.refs_2_.h_ref.refs_3_), custom_call_target="tpu_custom_call" | custom-call | flops 4294967296 | bytes 25165824 | tf_op jit(solution)/shard_map/pallas_call | solution.py:93
  135.8 1.5 collective-permute-done.1
  138.4 13.2 %shard_map.57 = f32[512,256]{1,0:T(8,128)} custom-call(bf16[4,512,8192]{2,1,0:T(8,128)(2,1)} %refs_1_.11, bf16[8192,256]{1,0:T(8,128)(2,1)} %all-gather.10.cloned.1.call-done.y_ref.refs_3_.refs_2_, bf16[4,512,8192]{2,1,0:T(8,128)(2,1)} %refs_1_.11, bf16[4,8192,256]{2,1,0:T(8,128)(2,1)} %all-gather.6.cloned.1.call-done.refs_4_.refs_2_.h_ref.refs_3_, ...), custom_call_target="tpu_custom_call" | custom-call | flops 4294967296 | bytes 25165824 | tf_op jit(solution)/shard_map/pallas_call | solution.py:118
  153.1 16.6 %shard_map.58 = f32[512,256]{1,0:T(8,128)} custom-call(bf16[4,512,8192]{2,1,0:T(8,128)(2,1)} %refs_1_.11, bf16[4,512,8192]{2,1,0:T(8,128)(2,1)} %refs_1_.11, bf16[4,512,8192]{2,1,0:T(8,128)(2,1)} %refs_1_.11, bf16[8192,256]{1,0:T(8,128)(2,1)} %all-gather.10.cloned.1.call-done.y_ref.refs_3_.refs_2_, ...), custom_call_target="tpu_custom_call" | custom-call | flops 6442450944 | bytes 37748736 | tf_op jit(solution)/shard_map/pallas_call | solution.py:157
  171.7 1.5 all-gather.8.cloned.1.call-done.y_ref.refs_2_
  173.2 7.3 %shard_map.59 = (bf16[512,256]{1,0:T(8,128)(2,1)}, f32[512,256]{1,0:T(8,128)}) custom-call(s32[1]{0:T(128)} %bitcast.5.flag_ref.refs_0_, bf16[4,512,8192]{2,1,0:T(8,128)(2,1)} %refs_1_.11, bf16[8192,256]{1,0:T(8,128)(2,1)} %all-gather.8.cloned.1.call-done.y_ref.refs_2_, f32[512,256]{1,0:T(8,128)} %fusion.1.base_ref, ...), custom_call_target="tpu_custom_call" | custom-call | flops 2147483648 | bytes 12582912 | tf_op jit(solution)/shard_map/pallas_call | solution.py:261
  180.7 1.4 collective-permute-start.3
  182.1 12.7 %shard_map.60.refs_4_ = f32[512,256]{1,0:T(8,128)} custom-call(bf16[4,512,8192]{2,1,0:T(8,128)(2,1)} %refs_1_.11, bf16[4,512,8192]{2,1,0:T(8,128)(2,1)} %refs_1_.11, bf16[8192,256]{1,0:T(8,128)(2,1)} %all-gather.10.cloned.1.call-done.y_ref.refs_3_.refs_2_, bf16[4,8192,256]{2,1,0:T(8,128)(2,1)} %all-gather.6.cloned.1.call-done.refs_4_.refs_2_.h_ref.refs_3_), custom_call_target="tpu_custom_call" | custom-call | flops 4294967296 | bytes 25165824 | tf_op jit(solution)/shard_map/pallas_call | solution.py:157
  195.7 13.3 %shard_map.61 = (f32[512,256]{1,0:T(8,128)}, f32[512,256]{1,0:T(8,128)}) custom-call(bf16[4,512,8192]{2,1,0:T(8,128)(2,1)} %refs_1_.11, bf16[4,512,8192]{2,1,0:T(8,128)(2,1)} %refs_1_.11, bf16[8192,256]{1,0:T(8,128)(2,1)} %all-gather.8.cloned.1.call-done.y_ref.refs_2_, f32[512,256]{1,0:T(8,128)} %broadcast_select_fusion.1.refs_3_, f32[512,256]{1,0:T(8,128)} %shard_map.60.refs_4_), custom_call_target="tpu_custom_call" | custom-call | flops 4294967296 | bytes 20971520 | tf_op jit(solution)/shard_map/pallas_call | solution.py:187
  209.0 1.9 add_select_fusion.1.base_ref
  211.0 5.5 %all-gather.12.cloned.1.call-done.y_ref.refs_1_ = bf16[8192,256]{1,0:T(8,128)(2,1)} async-done(((bf16[512,256]{1,0:T(8,128)(2,1)}), bf16[8192,256]{1,0:T(8,128)(2,1)}) %all-gather.12.cloned.1.call-update) | async-done | bytes 4194320 | tf_op jit(solution)/shard_map/all_gather | solution.py:283
  216.5 7.3 %shard_map.62 = (bf16[512,256]{1,0:T(8,128)(2,1)}, f32[512,256]{1,0:T(8,128)}) custom-call(s32[1]{0:T(128)} %bitcast.5.flag_ref.refs_0_, bf16[4,512,8192]{2,1,0:T(8,128)(2,1)} %refs_1_.11, bf16[8192,256]{1,0:T(8,128)(2,1)} %all-gather.12.cloned.1.call-done.y_ref.refs_1_, f32[512,256]{1,0:T(8,128)} %add_select_fusion.1.base_ref, ...), custom_call_target="tpu_custom_call" | custom-call | flops 2147483648 | bytes 12582912 | tf_op jit(solution)/shard_map/pallas_call | solution.py:261
  225.2 1.9 pad_maximum_fusion.1
  227.2 4.8 %collective-permute-start.4 = (bf16[3,512,256]{2,1,0:T(8,128)(2,1)}, bf16[3,512,256]{2,1,0:T(8,128)(2,1)S(1)}, u32[]{:S(2)}, u32[]{:S(2)}) collective-permute-start(bf16[3,512,256]{2,1,0:T(8,128)(2,1)} %pad_maximum_fusion.1), channel_id=1, source_target_pairs={{0,16},{1,17},{2,18},{3,19},{4,20},{5,21},{6,22},{7,23},{8,24},{9,... | collective-permute-start | bytes 2359304 | tf_op jit(solution)/shard_map/ppermute | solution.py:342
  232.0 9.4 %shard_map.63 = f32[512,256]{1,0:T(8,128)} custom-call(bf16[4,512,8192]{2,1,0:T(8,128)(2,1)} %refs_1_.11, bf16[8192,256]{1,0:T(8,128)(2,1)} %all-gather.12.cloned.1.call-done.y_ref.refs_1_, f32[512,256]{1,0:T(8,128)} %get-tuple-element.50.refs_2_), custom_call_target="tpu_custom_call" | custom-call | flops 2147483648 | bytes 12582912 | tf_op jit(solution)/shard_map/pallas_call | solution.py:187
  241.4 1.9 add_select_fusion.refs_3_
  243.3 14.8 %all-gather.14.cloned.1.call-done.refs_2_ = bf16[8192,256]{1,0:T(8,128)(2,1)} async-done(((bf16[512,256]{1,0:T(8,128)(2,1)}), bf16[8192,256]{1,0:T(8,128)(2,1)}) %all-gather.14.cloned.1.call-update) | async-done | bytes 4194320 | tf_op jit(solution)/shard_map/all_gather | solution.py:283
  258.1 7.2 %shard_map.64 = bf16[512,256]{1,0:T(8,128)(2,1)} custom-call(s32[1]{0:T(128)} %bitcast.5.flag_ref.refs_0_, bf16[4,512,8192]{2,1,0:T(8,128)(2,1)} %refs_1_.11, bf16[8192,256]{1,0:T(8,128)(2,1)} %all-gather.14.cloned.1.call-done.refs_2_, f32[512,256]{1,0:T(8,128)} %add_select_fusion.refs_3_, bf16[512,256]{1,0:T(8,128)(2,1)} %get-tuple-element.39.next_ref.refs_4_, ...), custom_call_target="tpu_custom_call" | custom-call | flops 2147483648 | bytes 12582912 | tf_op jit(solution)/shard_map/pallas_call | solution.py:261
  265.3 3.5 %collective-permute-start.6 = (bf16[512,256]{1,0:T(8,128)(2,1)}, bf16[512,256]{1,0:T(8,128)(2,1)S(1)}, u32[]{:S(2)}, u32[]{:S(2)}) collective-permute-start(bf16[512,256]{1,0:T(8,128)(2,1)} %shard_map.64), channel_id=1, source_target_pairs={{0,16},{1,17},{2,18},{3,19},{4,20},{5,21},{6,22},{7,23},{8,24},{9,... | collective-permute-start | bytes 786440 | tf_op jit(solution)/shard_map/ppermute | solution.py:343
  270.1 5.0 %collective-permute-done.6 = bf16[512,256]{1,0:T(8,128)(2,1)S(1)} collective-permute-done((bf16[512,256]{1,0:T(8,128)(2,1)}, bf16[512,256]{1,0:T(8,128)(2,1)S(1)}, u32[]{:S(2)}, u32[]{:S(2)}) %collective-permute-start.6) | collective-permute-done | bytes 262176 | tf_op jit(solution)/shard_map/ppermute | solution.py:343
  (49 shorter events, 12.8 us)
Async XLA Ops:
  6.5 94.2 %all-gather.6.cloned.1.call-start = ((), (), s32[]{:S(2)}) async-start(), calls=%async_computation | async-start | bytes 17825792 | tf_op jit(solution)/shard_map/all_gather | solution.py:283
  7.3 131.1 %all-gather.10.cloned.1.call-start = ((), (), s32[]{:S(2)}) async-start(), calls=%async_computation.2 | async-start | bytes 4456448 | tf_op jit(solution)/shard_map/all_gather | solution.py:283
  8.5 21.7 %collective-permute-start = (bf16[3,512,256]{2,1,0:T(8,128)(2,1)S(1)}, bf16[3,512,256]{2,1,0:T(8,128)(2,1)S(1)}, u32[]{:S(2)}, u32[]{:S(2)}) collective-permute-start(bf16[3,512,256]{2,1,0:T(8,128)(2,1)S(1)} %slice.19), channel_id=1, source_target_pairs={{0,16},{1,17},{2,18},{3,19},{4,20},{5,21},{6,22},{7,23},{8,24},{9,... | collective-permute-start | bytes 2359304 | tf_op jit(solution)/shard_map/ppermute | solution.py:296
  100.7 72.5 %all-gather.8.cloned.1.call-start = ((), (), s32[]{:S(2)}) async-start(), calls=%async_computation.1 | async-start | bytes 4456448 | tf_op jit(solution)/shard_map/all_gather | solution.py:283
  121.2 16.2 %collective-permute-start.1 = (f32[512,256]{1,0:T(8,128)}, f32[512,256]{1,0:T(8,128)S(1)}, u32[]{:S(2)}, u32[]{:S(2)}) collective-permute-start(f32[512,256]{1,0:T(8,128)} %shard_map.55), channel_id=1, source_target_pairs={{16,0},{17,1},{18,2},{19,3},{20,4},{21,5},{22,6},{23,7},{24,8},{25... | collective-permute-start | bytes 1572872 | tf_op jit(solution)/shard_map/ppermute | solution.py:302
  122.5 14.9 %copy-start.4 = (f32[512,256]{1,0:T(8,128)S(1)}, f32[512,256]{1,0:T(8,128)}, u32[]{:S(2)}) copy-start(f32[512,256]{1,0:T(8,128)} %shard_map.55) | copy-start | bytes 1572868
  122.5 14.9 %copy-start.6 = (f32[4,512,256]{2,1,0:T(8,128)S(1)}, f32[4,512,256]{2,1,0:T(8,128)}, u32[]{:S(2)}) copy-start(f32[4,512,256]{2,1,0:T(8,128)} %param.7) | copy-start | bytes 6291460
  122.5 14.9 %copy-start.8 = (f32[512]{0:T(512)S(1)}, f32[512]{0:T(512)}, u32[]{:S(2)}) copy-start(f32[512]{0:T(512)} %param.9) | copy-start | bytes 6148
  122.5 14.8 %copy-start.9 = (f32[512]{0:T(512)S(1)}, f32[512]{0:T(512)}, u32[]{:S(2)}) copy-start(f32[512]{0:T(512)} %param.8) | copy-start | bytes 6148
  138.3 78.2 %all-gather.12.cloned.1.call-start = ((), (), s32[]{:S(2)}) async-start(), calls=%async_computation.3 | async-start | bytes 4456448 | tf_op jit(solution)/shard_map/all_gather | solution.py:283
  151.7 19.1 %copy-start.5 = (f32[512,256]{1,0:T(8,128)S(1)}, f32[512,256]{1,0:T(8,128)}, u32[]{:S(2)}) copy-start(f32[512,256]{1,0:T(8,128)} %shard_map.57) | copy-start | bytes 1572868
  151.7 19.0 %collective-permute-start.2 = (f32[512,256]{1,0:T(8,128)}, f32[512,256]{1,0:T(8,128)S(1)}, u32[]{:S(2)}, u32[]{:S(2)}) collective-permute-start(f32[512,256]{1,0:T(8,128)} %shard_map.57), channel_id=1, source_target_pairs={{16,0},{17,1},{18,2},{19,3},{20,4},{21,5},{22,6},{23,7},{24,8},{25... | collective-permute-start | bytes 1572872 | tf_op jit(solution)/shard_map/ppermute | solution.py:313
  180.6 77.5 %all-gather.14.cloned.1.call-start = ((), (), s32[]{:S(2)}) async-start(), calls=%async_computation.4 | async-start | bytes 4456448 | tf_op jit(solution)/shard_map/all_gather | solution.py:283
  180.7 14.2 %copy-start = (f32[512,256]{1,0:T(8,128)S(1)}, f32[512,256]{1,0:T(8,128)}, u32[]{:S(2)}) copy-start(f32[512,256]{1,0:T(8,128)} %shard_map.58) | copy-start | bytes 1572868
  180.7 28.4 %collective-permute-start.3 = (f32[512,256]{1,0:T(8,128)}, f32[512,256]{1,0:T(8,128)S(1)}, u32[]{:S(2)}, u32[]{:S(2)}) collective-permute-start(f32[512,256]{1,0:T(8,128)} %get-tuple-element.42), channel_id=1, source_target_pairs={{16,0},{17,1},{18,2},{19,3},{20,4},{21,5},{22,6},{23,7},{24,8},{25... | collective-permute-start | bytes 1572872 | tf_op jit(solution)/shard_map/ppermute | solution.py:327
  211.0 14.2 %copy-start.1 = (bf16[512,256]{1,0:T(8,128)(2,1)S(1)}, bf16[512,256]{1,0:T(8,128)(2,1)}, u32[]{:S(2)}) copy-start(bf16[512,256]{1,0:T(8,128)(2,1)} %fusion.2) | copy-start | bytes 786436
  211.0 14.2 %copy-start.2 = (bf16[512,256]{1,0:T(8,128)(2,1)S(1)}, bf16[512,256]{1,0:T(8,128)(2,1)}, u32[]{:S(2)}) copy-start(bf16[512,256]{1,0:T(8,128)(2,1)} %get-tuple-element.41) | copy-start | bytes 786436
  223.9 17.4 %collective-permute-start.5 = (f32[512,256]{1,0:T(8,128)}, f32[512,256]{1,0:T(8,128)S(1)}, u32[]{:S(2)}, u32[]{:S(2)}) collective-permute-start(f32[512,256]{1,0:T(8,128)} %get-tuple-element.48), channel_id=1, source_target_pairs={{16,0},{17,1},{18,2},{19,3},{20,4},{21,5},{22,6},{23,7},{24,8},{25... | collective-permute-start | bytes 1572872 | tf_op jit(solution)/shard_map/ppermute | solution.py:327
  227.2 41.7 %collective-permute-start.4 = (bf16[3,512,256]{2,1,0:T(8,128)(2,1)}, bf16[3,512,256]{2,1,0:T(8,128)(2,1)S(1)}, u32[]{:S(2)}, u32[]{:S(2)}) collective-permute-start(bf16[3,512,256]{2,1,0:T(8,128)(2,1)} %pad_maximum_fusion.1), channel_id=1, source_target_pairs={{0,16},{1,17},{2,18},{3,19},{4,20},{5,21},{6,22},{7,23},{8,24},{9,... | collective-permute-start | bytes 2359304 | tf_op jit(solution)/shard_map/ppermute | solution.py:342
  243.3 25.6 %copy-start.3 = (bf16[512,256]{1,0:T(8,128)(2,1)S(1)}, bf16[512,256]{1,0:T(8,128)(2,1)}, u32[]{:S(2)}) copy-start(bf16[512,256]{1,0:T(8,128)(2,1)} %get-tuple-element.47) | copy-start | bytes 786436
  265.3 9.8 %copy-start.7 = (bf16[512,256]{1,0:T(8,128)(2,1)S(1)}, bf16[512,256]{1,0:T(8,128)(2,1)}, u32[]{:S(2)}) copy-start(bf16[512,256]{1,0:T(8,128)(2,1)} %shard_map.64) | copy-start | bytes 786436
  265.3 9.8 %collective-permute-start.6 = (bf16[512,256]{1,0:T(8,128)(2,1)}, bf16[512,256]{1,0:T(8,128)(2,1)S(1)}, u32[]{:S(2)}, u32[]{:S(2)}) collective-permute-start(bf16[512,256]{1,0:T(8,128)(2,1)} %shard_map.64), channel_id=1, source_target_pairs={{0,16},{1,17},{2,18},{3,19},{4,20},{5,21},{6,22},{7,23},{8,24},{9,... | collective-permute-start | bytes 786440 | tf_op jit(solution)/shard_map/ppermute | solution.py:343
Sparse Core Ops, SparseCore 0:
  8.9 91.7 all-gather.5
  102.3 34.9 all-gather.9
  138.9 34.2 all-gather.7
  180.7 35.7 all-gather.11
  224.0 34.0 all-gather.13

commit v6 on v4

--- a/solution.py
+++ b/solution.py
@@ -80,24 +80,27 @@
 
 
 def slots_kernel(count, *refs):
-    z_refs, h_ref, out_ref = refs[:count], refs[count], refs[count + 1]
-    total = dot(z_refs[0][0], h_ref[0])
+    z_refs, h_ref, out_ref = refs[:-2], refs[-2], refs[-1]
+    blocks = [z_ref.at[slot] for z_ref in z_refs for slot in range(z_ref.shape[0])]
+    total = dot(blocks[0][...], h_ref[0])
     for slot in range(1, count):
-        total += dot(z_refs[slot][0], h_ref[slot])
+        total += dot(blocks[slot][...], h_ref[slot])
     add_to(out_ref, total)
 
 
 def slots_product(pairs, z, h, shift, count):
     rows, columns, unknowns = shape = sizes(z, h)
     depth = unknowns // pairs
+    z_specs = [z_spec(rows, depth, slot) for slot in range(shift, shift + count)]
+    if shift == 0:
+        z_specs = [pl.BlockSpec((count, rows, depth), lambda k: (0, 0, k))]
     return call(
         functools.partial(slots_kernel, count), shape, count, count, count,
         grid=(pairs,),
-        in_specs=[z_spec(rows, depth, slot) for slot in range(shift, shift + count)]
-        + [h_spec(depth, columns, 0, count, pairs)],
+        in_specs=z_specs + [h_spec(depth, columns, 0, count, pairs)],
         out_specs=whole(rows, columns),
         out_shape=jax.ShapeDtypeStruct((rows, columns), jnp.float32),
-    )(*([z] * count), h)
+    )(*([z] * len(z_specs)), h)
 
 
 def next_kernel(z_new_ref, y_ref, z_old_ref, h_ref, part_ref, out_ref):
@@ -372,7 +375,7 @@
         slots, steps = lag_matrices.shape[0], excitation.shape[0]
         chosen = general_body
         depth = lag_matrices.shape[2] // members
-        if groups == 2 and members % 4 == 0 and depth % 128 == 0 and 2 < steps <= slots:
+        if groups == 2 and members % 4 == 0 and depth % 128 == 0 and 3 < steps <= slots:
             chosen = functools.partial(two_group_body, members // 2)
         return chosen(lag_matrices, history, excitation, admittance, saturation)
 

time: 283 us -> 283 us (level)
  no operation moved by 1% of the time
where the time goes in v6:
time: 283 us; the launch traced here: 282 us
  Pallas kernels  121 us (43%)
  waiting for transfers between devices  116 us (41%)
  starting transfers between devices  18.8 us (7%)
  between operations  13.4 us (5%)
  other arithmetic  10.5 us (4%)
  local copies, waits for them, and re-layouts  3.16 us (1%)
    all_gather x5, waiting for transfers between devices, gather_rows(): lax.all_gather(block, 'row', axis=axis, tiled=True, axis_index_groups=[or...  91.5 us
    pallas_call x2, Pallas kernels, slots_product(): call(functools.partial(slots_kernel, count), shape, count, count, count,...  33.6 us
    pallas_call x2, Pallas kernels, later_products(): call(functools.partial(later_kernel, rows, low, high, top), shape, produc...  29.4 us
    pallas_call x2, Pallas kernels, spread(): call(functools.partial(spread_kernel, rows, count), shape, count, count,...  22.7 us
    pallas_call x3, Pallas kernels, step(): call(functools.partial(step_kernel, pairs), shape, 1, 1, 1, in_specs=[pl....  22 us
    ppermute x1, waiting for transfers between devices, two_group_body(): incoming = lax.ppermute(history[slots - (steps - 1):], 'lag', up)  16.7 us
    pallas_call x1, Pallas kernels, next_product(): call(next_kernel, shape, 2, 2, 2, grid=(pairs,), in_specs=[z_spec(rows, d...  13.2 us
  transfers between devices with their start and end apart: 12, of which 7 were waited for; matrix products, arithmetic and copies ran while one was open for 5% of the time, Pallas kernels for 38%

profile of v6, /device:TPU:0, one launch (start us, length us, event | category | flops | bytes accessed | tf_op | source)
XLA Modules:
  0.0 282.4 jit_solution(2164385718470826480)
XLA Ops:
  8.5 4.9 %collective-permute-start = (bf16[3,512,256]{2,1,0:T(8,128)(2,1)S(1)}, bf16[3,512,256]{2,1,0:T(8,128)(2,1)S(1)}, u32[]{:S(2)}, u32[]{:S(2)}) collective-permute-start(bf16[3,512,256]{2,1,0:T(8,128)(2,1)S(1)} %slice.19), channel_id=1, source_target_pairs={{0,16},{1,17},{2,18},{3,19},{4,20},{5,21},{6,22},{7,23},{8,24},{9,... | collective-permute-start | bytes 2359304 | tf_op jit(solution)/shard_map/ppermute | solution.py:289
  13.4 16.7 %collective-permute-done = bf16[3,512,256]{2,1,0:T(8,128)(2,1)S(1)} collective-permute-done((bf16[3,512,256]{2,1,0:T(8,128)(2,1)S(1)}, bf16[3,512,256]{2,1,0:T(8,128)(2,1)S(1)}, u32[]{:S(2)}, u32[]{:S(2)}) %collective-permute-start) | collective-permute-done | bytes 786464 | tf_op jit(solution)/shard_map/ppermute | solution.py:289
  31.0 69.7 %all-gather.6.cloned.1.call-done.refs_1_.refs_2_.h_ref.refs_4_.refs_3_ = bf16[4,8192,256]{2,1,0:T(8,128)(2,1)} async-done(((bf16[4,512,256]{2,1,0:T(8,128)(2,1)}), bf16[4,8192,256]{2,1,0:T(8,128)(2,1)}) %all-gather.6.cloned.1.call-update) | async-done | bytes 16777232 | tf_op jit(solution)/shard_map/all_gather | solution.py:276
  100.8 20.2 %shard_map.55 = f32[512,256]{1,0:T(8,128)} custom-call(bf16[4,512,8192]{2,1,0:T(8,128)(2,1)} %z_ref.5, bf16[4,8192,256]{2,1,0:T(8,128)(2,1)} %all-gather.6.cloned.1.call-done.refs_1_.refs_2_.h_ref.refs_4_.refs_3_), custom_call_target="tpu_custom_call" | custom-call | flops 8589934592 | bytes 50331648 | tf_op jit(solution)/shard_map/pallas_call | solution.py:97
  122.4 13.3 %shard_map.56.part_ref = f32[512,256]{1,0:T(8,128)} custom-call(bf16[4,512,8192]{2,1,0:T(8,128)(2,1)} %z_ref.5, bf16[4,512,8192]{2,1,0:T(8,128)(2,1)} %z_ref.5, bf16[4,8192,256]{2,1,0:T(8,128)(2,1)} %all-gather.6.cloned.1.call-done.refs_1_.refs_2_.h_ref.refs_4_.refs_3_), custom_call_target="tpu_custom_call" | custom-call | flops 4294967296 | bytes 25165824 | tf_op jit(solution)/shard_map/pallas_call | solution.py:97
  135.7 1.5 collective-permute-done.1
  138.3 13.2 %shard_map.57 = f32[512,256]{1,0:T(8,128)} custom-call(bf16[4,512,8192]{2,1,0:T(8,128)(2,1)} %z_ref.5, bf16[8192,256]{1,0:T(8,128)(2,1)} %all-gather.10.cloned.1.call-done.y_ref.refs_3_.refs_2_, bf16[4,512,8192]{2,1,0:T(8,128)(2,1)} %z_ref.5, bf16[4,8192,256]{2,1,0:T(8,128)(2,1)} %all-gather.6.cloned.1.call-done.refs_1_.refs_2_.h_ref.refs_4_.refs_3_, ...), custom_call_target="tpu_custom_call" | custom-call | flops 4294967296 | bytes 25165824 | tf_op jit(solution)/shard_map/pallas_call | solution.py:121
  153.0 16.6 %shard_map.58 = f32[512,256]{1,0:T(8,128)} custom-call(bf16[4,512,8192]{2,1,0:T(8,128)(2,1)} %z_ref.5, bf16[4,512,8192]{2,1,0:T(8,128)(2,1)} %z_ref.5, bf16[4,512,8192]{2,1,0:T(8,128)(2,1)} %z_ref.5, bf16[8192,256]{1,0:T(8,128)(2,1)} %all-gather.10.cloned.1.call-done.y_ref.refs_3_.refs_2_, ...), custom_call_target="tpu_custom_call" | custom-call | flops 6442450944 | bytes 37748736 | tf_op jit(solution)/shard_map/pallas_call | solution.py:160
  171.6 1.5 all-gather.8.cloned.1.call-done.y_ref.refs_2_
  173.1 7.4 %shard_map.59 = (f32[512,256]{1,0:T(8,128)}, bf16[512,256]{1,0:T(8,128)(2,1)}) custom-call(s32[1]{0:T(128)} %bitcast.5.flag_ref, bf16[4,512,8192]{2,1,0:T(8,128)(2,1)} %z_ref.5, bf16[8192,256]{1,0:T(8,128)(2,1)} %all-gather.8.cloned.1.call-done.y_ref.refs_2_, f32[512,256]{1,0:T(8,128)} %fusion.1.base_ref, bf16[512,256]{1,0:T(8,128)(2,1)} %get-tuple-element.40.next_ref, ...), custom_call_target="tpu_custom_call" | custom-call | flops 2147483648 | bytes 12582912 | tf_op jit(solution)/shard_map/pallas_call | solution.py:251
  180.6 1.4 collective-permute-start.3
  182.0 12.8 %shard_map.60.refs_4_ = f32[512,256]{1,0:T(8,128)} custom-call(bf16[4,512,8192]{2,1,0:T(8,128)(2,1)} %z_ref.5, bf16[4,512,8192]{2,1,0:T(8,128)(2,1)} %z_ref.5, bf16[8192,256]{1,0:T(8,128)(2,1)} %all-gather.10.cloned.1.call-done.y_ref.refs_3_.refs_2_, bf16[4,8192,256]{2,1,0:T(8,128)(2,1)} %all-gather.6.cloned.1.call-done.refs_1_.refs_2_.h_ref.refs_4_.refs_3_), custom_call_target="tpu_custom_call" | custom-call | flops 4294967296 | bytes 25165824 | tf_op jit(solution)/shard_map/pallas_call | solution.py:160
  195.6 13.3 %shard_map.61 = (f32[512,256]{1,0:T(8,128)}, f32[512,256]{1,0:T(8,128)}) custom-call(bf16[4,512,8192]{2,1,0:T(8,128)(2,1)} %z_ref.5, bf16[4,512,8192]{2,1,0:T(8,128)(2,1)} %z_ref.5, bf16[8192,256]{1,0:T(8,128)(2,1)} %all-gather.8.cloned.1.call-done.y_ref.refs_2_, f32[512,256]{1,0:T(8,128)} %broadcast_select_fusion.1.refs_3_, f32[512,256]{1,0:T(8,128)} %shard_map.60.refs_4_), custom_call_target="tpu_custom_call" | custom-call | flops 4294967296 | bytes 20971520 | tf_op jit(solution)/shard_map/pallas_call | solution.py:190
  208.9 1.9 add_select_fusion.1.base_ref
  210.9 5.5 %all-gather.12.cloned.1.call-done.y_ref.refs_1_ = bf16[8192,256]{1,0:T(8,128)(2,1)} async-done(((bf16[512,256]{1,0:T(8,128)(2,1)}), bf16[8192,256]{1,0:T(8,128)(2,1)}) %all-gather.12.cloned.1.call-update) | async-done | bytes 4194320 | tf_op jit(solution)/shard_map/all_gather | solution.py:276
  216.4 7.3 %shard_map.62 = (f32[512,256]{1,0:T(8,128)}, bf16[512,256]{1,0:T(8,128)(2,1)}) custom-call(s32[1]{0:T(128)} %bitcast.5.flag_ref, bf16[4,512,8192]{2,1,0:T(8,128)(2,1)} %z_ref.5, bf16[8192,256]{1,0:T(8,128)(2,1)} %all-gather.12.cloned.1.call-done.y_ref.refs_1_, f32[512,256]{1,0:T(8,128)} %add_select_fusion.1.base_ref, ...), custom_call_target="tpu_custom_call" | custom-call | flops 2147483648 | bytes 12582912 | tf_op jit(solution)/shard_map/pallas_call | solution.py:251
  225.1 1.9 pad_maximum_fusion.1
  227.0 4.8 %collective-permute-start.4 = (bf16[3,512,256]{2,1,0:T(8,128)(2,1)}, bf16[3,512,256]{2,1,0:T(8,128)(2,1)S(1)}, u32[]{:S(2)}, u32[]{:S(2)}) collective-permute-start(bf16[3,512,256]{2,1,0:T(8,128)(2,1)} %pad_maximum_fusion.1), channel_id=1, source_target_pairs={{0,16},{1,17},{2,18},{3,19},{4,20},{5,21},{6,22},{7,23},{8,24},{9,... | collective-permute-start | bytes 2359304 | tf_op jit(solution)/shard_map/ppermute | solution.py:335
  231.8 9.4 %shard_map.63 = f32[512,256]{1,0:T(8,128)} custom-call(bf16[4,512,8192]{2,1,0:T(8,128)(2,1)} %z_ref.5, bf16[8192,256]{1,0:T(8,128)(2,1)} %all-gather.12.cloned.1.call-done.y_ref.refs_1_, f32[512,256]{1,0:T(8,128)} %get-tuple-element.51.refs_2_), custom_call_target="tpu_custom_call" | custom-call | flops 2147483648 | bytes 12582912 | tf_op jit(solution)/shard_map/pallas_call | solution.py:190
  241.2 1.9 add_select_fusion.base_ref
  243.1 14.8 %all-gather.14.cloned.1.call-done.y_ref = bf16[8192,256]{1,0:T(8,128)(2,1)} async-done(((bf16[512,256]{1,0:T(8,128)(2,1)}), bf16[8192,256]{1,0:T(8,128)(2,1)}) %all-gather.14.cloned.1.call-update) | async-done | bytes 4194320 | tf_op jit(solution)/shard_map/all_gather | solution.py:276
  257.9 7.3 %shard_map.64 = (f32[512,256]{1,0:T(8,128)}, bf16[512,256]{1,0:T(8,128)(2,1)}) custom-call(s32[1]{0:T(128)} %bitcast.5.flag_ref, bf16[4,512,8192]{2,1,0:T(8,128)(2,1)} %z_ref.5, bf16[8192,256]{1,0:T(8,128)(2,1)} %all-gather.14.cloned.1.call-done.y_ref, f32[512,256]{1,0:T(8,128)} %add_select_fusion.base_ref, bf16[512,256]{1,0:T(8,128)(2,1)} %get-tuple-element.40.next_ref, ...), custom_call_target="tpu_custom_call" | custom-call | flops 2147483648 | bytes 12582912 | tf_op jit(solution)/shard_map/pallas_call | solution.py:251
  265.3 3.5 %collective-permute-start.6 = (bf16[512,256]{1,0:T(8,128)(2,1)}, bf16[512,256]{1,0:T(8,128)(2,1)S(1)}, u32[]{:S(2)}, u32[]{:S(2)}) collective-permute-start(bf16[512,256]{1,0:T(8,128)(2,1)} %get-tuple-element.52), channel_id=1, source_target_pairs={{0,16},{1,17},{2,18},{3,19},{4,20},{5,21},{6,22},{7,23},{8,24},{9,... | collective-permute-start | bytes 786440 | tf_op jit(solution)/shard_map/ppermute | solution.py:336
  270.1 5.0 %collective-permute-done.6 = bf16[512,256]{1,0:T(8,128)(2,1)S(1)} collective-permute-done((bf16[512,256]{1,0:T(8,128)(2,1)}, bf16[512,256]{1,0:T(8,128)(2,1)S(1)}, u32[]{:S(2)}, u32[]{:S(2)}) %collective-permute-start.6) | collective-permute-done | bytes 262176 | tf_op jit(solution)/shard_map/ppermute | solution.py:336
  (49 shorter events, 12.8 us)
Async XLA Ops:
  6.5 94.2 %all-gather.6.cloned.1.call-start = ((), (), s32[]{:S(2)}) async-start(), calls=%async_computation | async-start | bytes 17825792 | tf_op jit(solution)/shard_map/all_gather | solution.py:276
  7.3 131.0 %all-gather.10.cloned.1.call-start = ((), (), s32[]{:S(2)}) async-start(), calls=%async_computation.2 | async-start | bytes 4456448 | tf_op jit(solution)/shard_map/all_gather | solution.py:276
  8.5 21.7 %collective-permute-start = (bf16[3,512,256]{2,1,0:T(8,128)(2,1)S(1)}, bf16[3,512,256]{2,1,0:T(8,128)(2,1)S(1)}, u32[]{:S(2)}, u32[]{:S(2)}) collective-permute-start(bf16[3,512,256]{2,1,0:T(8,128)(2,1)S(1)} %slice.19), channel_id=1, source_target_pairs={{0,16},{1,17},{2,18},{3,19},{4,20},{5,21},{6,22},{7,23},{8,24},{9,... | collective-permute-start | bytes 2359304 | tf_op jit(solution)/shard_map/ppermute | solution.py:289
  100.7 72.4 %all-gather.8.cloned.1.call-start = ((), (), s32[]{:S(2)}) async-start(), calls=%async_computation.1 | async-start | bytes 4456448 | tf_op jit(solution)/shard_map/all_gather | solution.py:276
  121.0 16.2 %collective-permute-start.1 = (f32[512,256]{1,0:T(8,128)}, f32[512,256]{1,0:T(8,128)S(1)}, u32[]{:S(2)}, u32[]{:S(2)}) collective-permute-start(f32[512,256]{1,0:T(8,128)} %shard_map.55), channel_id=1, source_target_pairs={{16,0},{17,1},{18,2},{19,3},{20,4},{21,5},{22,6},{23,7},{24,8},{25... | collective-permute-start | bytes 1572872 | tf_op jit(solution)/shard_map/ppermute | solution.py:295
  122.3 14.9 %copy-start.4 = (f32[512,256]{1,0:T(8,128)S(1)}, f32[512,256]{1,0:T(8,128)}, u32[]{:S(2)}) copy-start(f32[512,256]{1,0:T(8,128)} %shard_map.55) | copy-start | bytes 1572868
  122.3 14.9 %copy-start.6 = (f32[4,512,256]{2,1,0:T(8,128)S(1)}, f32[4,512,256]{2,1,0:T(8,128)}, u32[]{:S(2)}) copy-start(f32[4,512,256]{2,1,0:T(8,128)} %param.7) | copy-start | bytes 6291460
  122.4 14.9 %copy-start.8 = (f32[512]{0:T(512)S(1)}, f32[512]{0:T(512)}, u32[]{:S(2)}) copy-start(f32[512]{0:T(512)} %param.9) | copy-start | bytes 6148
  122.4 14.9 %copy-start.9 = (f32[512]{0:T(512)S(1)}, f32[512]{0:T(512)}, u32[]{:S(2)}) copy-start(f32[512]{0:T(512)} %param.8) | copy-start | bytes 6148
  138.2 78.2 %all-gather.12.cloned.1.call-start = ((), (), s32[]{:S(2)}) async-start(), calls=%async_computation.3 | async-start | bytes 4456448 | tf_op jit(solution)/shard_map/all_gather | solution.py:276
  151.5 19.1 %copy-start.5 = (f32[512,256]{1,0:T(8,128)S(1)}, f32[512,256]{1,0:T(8,128)}, u32[]{:S(2)}) copy-start(f32[512,256]{1,0:T(8,128)} %shard_map.57) | copy-start | bytes 1572868
  151.5 19.0 %collective-permute-start.2 = (f32[512,256]{1,0:T(8,128)}, f32[512,256]{1,0:T(8,128)S(1)}, u32[]{:S(2)}, u32[]{:S(2)}) collective-permute-start(f32[512,256]{1,0:T(8,128)} %shard_map.57), channel_id=1, source_target_pairs={{16,0},{17,1},{18,2},{19,3},{20,4},{21,5},{22,6},{23,7},{24,8},{25... | collective-permute-start | bytes 1572872 | tf_op jit(solution)/shard_map/ppermute | solution.py:306
  180.5 77.4 %all-gather.14.cloned.1.call-start = ((), (), s32[]{:S(2)}) async-start(), calls=%async_computation.4 | async-start | bytes 4456448 | tf_op jit(solution)/shard_map/all_gather | solution.py:276
  180.5 14.2 %copy-start = (f32[512,256]{1,0:T(8,128)S(1)}, f32[512,256]{1,0:T(8,128)}, u32[]{:S(2)}) copy-start(f32[512,256]{1,0:T(8,128)} %shard_map.58) | copy-start | bytes 1572868
  180.6 28.4 %collective-permute-start.3 = (f32[512,256]{1,0:T(8,128)}, f32[512,256]{1,0:T(8,128)S(1)}, u32[]{:S(2)}, u32[]{:S(2)}) collective-permute-start(f32[512,256]{1,0:T(8,128)} %get-tuple-element.43), channel_id=1, source_target_pairs={{16,0},{17,1},{18,2},{19,3},{20,4},{21,5},{22,6},{23,7},{24,8},{25... | collective-permute-start | bytes 1572872 | tf_op jit(solution)/shard_map/ppermute | solution.py:320
  210.9 14.2 %copy-start.1 = (bf16[512,256]{1,0:T(8,128)(2,1)S(1)}, bf16[512,256]{1,0:T(8,128)(2,1)}, u32[]{:S(2)}) copy-start(bf16[512,256]{1,0:T(8,128)(2,1)} %fusion.2) | copy-start | bytes 786436
  210.9 14.2 %copy-start.2 = (bf16[512,256]{1,0:T(8,128)(2,1)S(1)}, bf16[512,256]{1,0:T(8,128)(2,1)}, u32[]{:S(2)}) copy-start(bf16[512,256]{1,0:T(8,128)(2,1)} %get-tuple-element.42) | copy-start | bytes 786436
  223.7 17.5 %collective-permute-start.5 = (f32[512,256]{1,0:T(8,128)}, f32[512,256]{1,0:T(8,128)S(1)}, u32[]{:S(2)}, u32[]{:S(2)}) collective-permute-start(f32[512,256]{1,0:T(8,128)} %get-tuple-element.49), channel_id=1, source_target_pairs={{16,0},{17,1},{18,2},{19,3},{20,4},{21,5},{22,6},{23,7},{24,8},{25... | collective-permute-start | bytes 1572872 | tf_op jit(solution)/shard_map/ppermute | solution.py:320
  227.0 41.8 %collective-permute-start.4 = (bf16[3,512,256]{2,1,0:T(8,128)(2,1)}, bf16[3,512,256]{2,1,0:T(8,128)(2,1)S(1)}, u32[]{:S(2)}, u32[]{:S(2)}) collective-permute-start(bf16[3,512,256]{2,1,0:T(8,128)(2,1)} %pad_maximum_fusion.1), channel_id=1, source_target_pairs={{0,16},{1,17},{2,18},{3,19},{4,20},{5,21},{6,22},{7,23},{8,24},{9,... | collective-permute-start | bytes 2359304 | tf_op jit(solution)/shard_map/ppermute | solution.py:335
  243.1 25.7 %copy-start.3 = (bf16[512,256]{1,0:T(8,128)(2,1)S(1)}, bf16[512,256]{1,0:T(8,128)(2,1)}, u32[]{:S(2)}) copy-start(bf16[512,256]{1,0:T(8,128)(2,1)} %get-tuple-element.48) | copy-start | bytes 786436
  265.3 9.8 %copy-start.7 = (bf16[512,256]{1,0:T(8,128)(2,1)S(1)}, bf16[512,256]{1,0:T(8,128)(2,1)}, u32[]{:S(2)}) copy-start(bf16[512,256]{1,0:T(8,128)(2,1)} %get-tuple-element.52) | copy-start | bytes 786436
  265.3 9.8 %collective-permute-start.6 = (bf16[512,256]{1,0:T(8,128)(2,1)}, bf16[512,256]{1,0:T(8,128)(2,1)S(1)}, u32[]{:S(2)}, u32[]{:S(2)}) collective-permute-start(bf16[512,256]{1,0:T(8,128)(2,1)} %get-tuple-element.52), channel_id=1, source_target_pairs={{0,16},{1,17},{2,18},{3,19},{4,20},{5,21},{6,22},{7,23},{8,24},{9,... | collective-permute-start | bytes 786440 | tf_op jit(solution)/shard_map/ppermute | solution.py:336
Sparse Core Ops, SparseCore 0:
  8.9 91.7 all-gather.5
  102.3 34.9 all-gather.9
  138.9 34.1 all-gather.7
  180.6 35.7 all-gather.11
  223.9 34.0 all-gather.13
